TPU v7x, 32 devices: a whole 2x2x4 slice. The times are simulated.
32 devices in a mesh: layer: 4 (over x, core), doc: 8 (over z, y).
Axes of the slice: x: 2, y: 2, z: 4, core: 2. Of those that a mesh axis runs over, the one named last changes fastest.
Arguments:
- query_grads: bfloat16 [4, 256, 4096], P('layer', 'doc'), may hold values from -6 to 6
- stored_grads: bfloat16 [4, 8192, 4096], P('layer', 'doc'), may hold values from -0.0234375 to 0.0234375
- basis_in: float32 [4, 64, 64], P('layer'), may hold values from -0.75 to 0.75
- basis_out: float32 [4, 64, 64], P('layer'), may hold values from -0.75 to 0.75
- eigen_values: float32 [4, 64, 64], P('layer'), may hold values from 0.02 to 4
- layer_mask: int32 [256, 4], P(None, 'layer'), may hold values 0 or 1
- doc_counts: int32 [8], P('doc'), may hold values from 1 to 1024, 4096 in all
Outputs:
- scores: float32 [256, 8192], P('layer', 'doc')
Inputs may be any that keep to these rules, and one draw needn't show every extreme that they name: `doc_counts`: the counts sum to 4096 and the largest equals 1024.
All inputs are finite; a program needn't handle non-finite values. No bound on the sum of `layer_mask` or of `doc_counts` on one device may be relied on, other than what follows from the above.
Results may differ from a plain program's by a relative error of at most 0.0029.
Values may be sent and summed in bfloat16 or wider, within the bound.
A program may use at most 64 MiB of HBM per device.

v0:
```python
import jax
import jax.numpy as jnp
from jax import lax
from jax.sharding import PartitionSpec as P

damping = 0.1


def precondition(gradients, basis_in, basis_out, eigen_values):
    row_count = gradients.shape[0]
    grid_blocks = gradients.astype(jnp.float32).reshape(
        row_count, basis_out.shape[0], basis_in.shape[0]
    )
    rotated = jnp.einsum(
        "xi,qxy,yj->qij", basis_out, grid_blocks, basis_in, precision=lax.Precision.HIGHEST
    )
    scaled = rotated / (eigen_values + damping)
    restored = jnp.einsum(
        "bi,qij,aj->qba", basis_out, scaled, basis_in, precision=lax.Precision.HIGHEST
    )
    return restored.reshape(row_count, -1).astype(jnp.bfloat16)


def on_device(query_grads, stored_grads, basis_in, basis_out, eigen_values, layer_mask, doc_counts):
    stored = stored_grads[0]
    base_in = basis_in[0]
    base_out = basis_out[0]
    eigens = eigen_values[0]
    row_weights = layer_mask[:, 0].astype(jnp.bfloat16)
    own_rows = precondition(query_grads[0], base_in, base_out, eigens)
    masked = lax.all_gather(own_rows, "doc", axis=0, tiled=True) * row_weights[:, None]
    score_tiles = lax.dot_general(
        masked, stored, (((1,), (1,)), ((), ())), preferred_element_type=jnp.float32
    )
    live_slots = jnp.arange(stored.shape[0], dtype=jnp.int32) < doc_counts[0]
    score_tiles = jnp.where(live_slots[None, :], score_tiles, jnp.zeros_like(score_tiles))
    return lax.psum_scatter(score_tiles, "layer", scatter_dimension=0, tiled=True)


def solution(mesh):
    in_specs = (
        P("layer", "doc", None),
        P("layer", "doc", None),
        P("layer", None, None),
        P("layer", None, None),
        P("layer", None, None),
        P(None, "layer"),
        P("doc"),
    )
    out_specs = P("layer", "doc")
    return jax.shard_map(
        on_device, mesh=mesh, in_specs=in_specs, out_specs=out_specs, check_vma=False
    )
```

profile of v0, /device:TPU:24, one launch (start us, length us, event | category | flops | bytes accessed | tf_op | source)
XLA Modules:
  0.0 102.8 jit_solution(17964470277720270904)
XLA Ops:
  6.5 0.0 copy-start
  6.5 0.0 copy-start.1
  6.5 0.0 all-gather.2.cloned.1.call-start
  6.5 0.8 add_bitcast_fusion
  7.3 1.5 %reshape.10 = bf16[32,64,64]{2,1,0:T(8,128)(2,1)S(1)} reshape(bf16[1,32,4096]{2,1,0:T(8,128)(2,1)} %param.7) | data formatting | bytes 524288 | tf_op jit(solution)/shard_map/reshape | solution.py:11
  8.8 0.0 copy-done
  8.8 0.7 fusion.13
  9.5 0.0 copy-done.1
  9.5 1.8 %convolution_divide_fusion = f32[32,64,64]{2,1,0:T(8,128)S(1)} fusion(f32[32,64,64]{2,1,0:T(8,128)S(1)} %fusion.13, f32[64,64]{1,0:T(8,128)S(1)} %add_bitcast_fusion, f32[1,64,64]{2,1,0:T(8,128)S(1)} %copy-done.1), kind=kOutput, calls=%fused_computation.3 | convolution fusion | flops 100794368 | bytes 1081344 | tf_op jit(solution)/shard_map/xi,qxy,yj->qij/dot_general | solution.py:14
  11.3 0.0 copy-start.2
  11.3 1.1 %fusion.11 = f32[32,64,64]{1,2,0:T(8,128)S(1)} fusion(f32[32,64,64]{2,1,0:T(8,128)S(1)} %convolution_divide_fusion, f32[1,64,64]{2,1,0:T(8,128)S(1)} %copy-done), kind=kOutput, calls=%fused_computation.9 | convolution fusion | flops 100663296 | bytes 1064960 | tf_op jit(solution)/shard_map/bi,qij,aj->qba/dot_general | solution.py:18
  12.4 1.0 convolution_convert_fusion
  13.4 1.2 %convert_element_type.12 = bf16[32,4096]{1,0:T(8,128)(2,1)} reshape(bf16[32,64,64]{2,1,0:T(8,128)(2,1)S(1)} %convolution_convert_fusion) | data formatting | bytes 524288 | tf_op jit(solution)/shard_map/convert_element_type | solution.py:21
  14.5 0.0 all-gather.2.cloned.1.call-update
  14.6 0.0 reduce-scatter.2.cloned.1.call-start
  15.3 0.0 copy-done.2
  15.3 48.2 %all-gather.2.cloned.1.call-done = bf16[256,4096]{1,0:T(8,128)(2,1)} async-done(((bf16[32,4096]{1,0:T(8,128)(2,1)}), bf16[256,4096]{1,0:T(8,128)(2,1)}) %all-gather.2.cloned.1.call-update) | async-done | bytes 2097168 | tf_op jit(solution)/shard_map/all_gather | solution.py:31
  63.5 7.4 %fusion.3 = f32[256,1024]{1,0:T(8,128)} fusion(bf16[1,1024,4096]{2,1,0:T(8,128)(2,1)} %param.8, bf16[256,4096]{1,0:T(8,128)(2,1)} %all-gather.2.cloned.1.call-done, bf16[256]{0:T(256)(128)(2,1)S(1)} %convert_reduce_fusion, pred[1024]{0:T(1024)(128)(4,1)S(1)} %iota_compare_fusion), kind=kOutput, calls=%fused_computation.5 | convolution fusion | flops 2148794368 | bytes 11535872 | tf_op jit(solution)/shard_map/dot_general | solution.py:32
  70.9 0.0 reduce-scatter.2.cloned.1.call-update
  70.9 25.0 %reduce-scatter.2.cloned.1.call-done = f32[64,1024]{1,0:T(8,128)} async-done(((f32[256,1024]{1,0:T(8,128)}), f32[64,1024]{1,0:T(8,128)}) %reduce-scatter.2.cloned.1.call-update) | async-done | bytes 262160 | tf_op jit(solution)/shard_map/reduce_scatter | solution.py:37
  (2 shorter events, 0.0 us)
Async XLA Ops:
  6.5 2.3 %copy-start = (f32[1,64,64]{2,1,0:T(8,128)S(1)}, f32[1,64,64]{2,1,0:T(8,128)}, u32[]{:S(2)}) copy-start(f32[1,64,64]{2,1,0:T(8,128)} %param.10) | copy-start | bytes 49156
  6.5 2.9 %copy-start.1 = (f32[1,64,64]{2,1,0:T(8,128)S(1)}, f32[1,64,64]{2,1,0:T(8,128)}, u32[]{:S(2)}) copy-start(f32[1,64,64]{2,1,0:T(8,128)} %param.9) | copy-start | bytes 49156
  6.5 56.9 %all-gather.2.cloned.1.call-start = ((), (), s32[]{:S(2)}) async-start(), calls=%async_computation.1 | async-start | bytes 2359296 | tf_op jit(solution)/shard_map/all_gather | solution.py:31
  11.3 4.0 %copy-start.2 = (s32[256,1]{0,1:T(1,128)S(1)}, s32[256,1]{0,1:T(1,128)}, u32[]{:S(2)}) copy-start(s32[256,1]{0,1:T(1,128)} %param.12) | copy-start | bytes 3076
  14.6 81.4 %reduce-scatter.2.cloned.1.call-start = ((), (), s32[]{:S(2)}) async-start(), calls=%async_computation.2 | async-start | bytes 1310720 | tf_op jit(solution)/shard_map/reduce_scatter | solution.py:37
Sparse Core Ops, SparseCore 0:
  14.7 48.7 all-gather.1
  71.0 24.8 reduce-scatter.1
where the time goes:
time: 105 us; the launch traced here: 103 us
  waiting for transfers between devices  73.2 us (70%)
  between operations  14.1 us (13%)
  matrix products  11.9 us (11%)
  local copies, waits for them, and re-layouts  2.66 us (3%)
    all_gather x1, waiting for transfers between devices, on_device(): lax.all_gather(own_rows, 'doc', axis=0, tiled=True) * row_weights[:, None]  48.2 us
    reduce_scatter x1, waiting for transfers between devices, on_device(): lax.psum_scatter(score_tiles, 'layer', scatter_dimension=0, tiled=True)  25 us
    dot_general x1, matrix products, on_device(): lax.dot_general(masked, stored, (((1,), (1,)), ((), ())), preferred_eleme...  7.39 us
    dot_general x2, matrix products, precondition(): jnp.einsum('xi,qxy,yj->qij', basis_out, grid_blocks, basis_in, precision=...  2.47 us
  transfers between devices with their start and end apart: 2, of which 2 were waited for; matrix products, arithmetic and copies ran while one was open for 0% of the time, Pallas kernels for 0%

commit v1 on v0

--- a/solution.py
+++ b/solution.py
@@ -1,9 +1,16 @@
+import functools
 import jax
 import jax.numpy as jnp
 from jax import lax
+from jax.experimental import pallas as pl
+from jax.experimental.pallas import tpu as pltpu
 from jax.sharding import PartitionSpec as P
 
 damping = 0.1
+N_CHUNK = 4
+MESH = pl.DeviceIdType.MESH
+f32 = jnp.float32
+bf16 = jnp.bfloat16
 
 
 def precondition(gradients, basis_in, basis_out, eigen_values):
@@ -21,13 +28,10 @@
     return restored.reshape(row_count, -1).astype(jnp.bfloat16)
 
 
-def on_device(query_grads, stored_grads, basis_in, basis_out, eigen_values, layer_mask, doc_counts):
+def by_collectives(query_grads, stored_grads, basis_in, basis_out, eigen_values, layer_mask, doc_counts):
     stored = stored_grads[0]
-    base_in = basis_in[0]
-    base_out = basis_out[0]
-    eigens = eigen_values[0]
     row_weights = layer_mask[:, 0].astype(jnp.bfloat16)
-    own_rows = precondition(query_grads[0], base_in, base_out, eigens)
+    own_rows = precondition(query_grads[0], basis_in[0], basis_out[0], eigen_values[0])
     masked = lax.all_gather(own_rows, "doc", axis=0, tiled=True) * row_weights[:, None]
     score_tiles = lax.dot_general(
         masked, stored, (((1,), (1,)), ((), ())), preferred_element_type=jnp.float32
@@ -35,6 +39,294 @@
     live_slots = jnp.arange(stored.shape[0], dtype=jnp.int32) < doc_counts[0]
     score_tiles = jnp.where(live_slots[None, :], score_tiles, jnp.zeros_like(score_tiles))
     return lax.psum_scatter(score_tiles, "layer", scatter_dimension=0, tiled=True)
+
+
+def halves(x):
+    hi = x.astype(bf16)
+    return hi, (x - hi.astype(f32)).astype(bf16)
+
+
+def nn(a, b):
+    return lax.dot_general(a, b, (((1,), (0,)), ((), ())), preferred_element_type=f32)
+
+
+def nt(a, b):
+    return lax.dot_general(a, b, (((1,), (1,)), ((), ())), preferred_element_type=f32)
+
+
+def one_hot(hits):
+    return jnp.where(hits, 1.0, 0.0).astype(bf16)
+
+
+def iota(shape, dim):
+    return lax.broadcasted_iota(jnp.int32, shape, dim)
+
+
+def write_own_rows(q_ref, bi_ref, bo_ref, ev_ref, mask_ref, gath, me):
+    x = q_ref[0].astype(f32)
+    r, c = iota((256, 256), 0), iota((256, 256), 1)
+    same = (r // 128 == (c // 64) % 2) & ((r // 64) % 2 == c // 128)
+    put_a = one_hot(iota((256, 64), 0) % 64 == iota((256, 64), 1))
+    wa = [
+        jnp.where(same, nt(nn(put_a, part).astype(bf16), put_a), 0.0).astype(bf16)
+        for part in halves(bi_ref[0])
+    ]
+    row = iota((512, 64), 0)
+    put_b = one_hot(2 * ((row // 8) % 32) + row // 256 == iota((512, 64), 1))
+    eye = iota((512, 512), 0) % 8 == iota((512, 512), 1) % 8
+    wc, wb = [], []
+    for part in halves(bo_ref[0]):
+        wc.append(jnp.where(eye, nt(nn(put_b, part).astype(bf16), put_b), 0.0).astype(bf16))
+        wb.append(jnp.where(eye, nt(nt(put_b, part).astype(bf16), put_b), 0.0).astype(bf16))
+    inverse = 1.0 / (ev_ref[0] + damping)
+    top, low = halves(inverse)
+    low = inverse - top.astype(f32)
+    mid, low = halves(low)
+    scale = 0.0
+    for part in (top, mid, low):
+        scale = scale + nt(nn(put_b, part).astype(bf16), put_a)
+
+    turned = []
+    for gp in range(2):
+        pieces = [
+            jnp.concatenate(
+                [
+                    x[8 * (2 * gp + g) : 8 * (2 * gp + g) + 8, 128 * j : 128 * j + 128]
+                    for j in range(32)
+                ],
+                axis=0,
+            )
+            for g in range(2)
+        ]
+        block = jnp.concatenate(pieces, axis=1).astype(bf16)
+        turned.append(nn(block, wa[0]) + nn(block, wa[1]))
+    s = jnp.concatenate(
+        [
+            jnp.concatenate([turned[gp][:, 128 * p : 128 * p + 128] for gp in range(2)], axis=1)
+            for p in range(2)
+        ],
+        axis=0,
+    )
+    s_hi, s_lo = halves(s)
+    rotated = nn(wb[0], s_hi) + (nn(wb[0], s_lo) + nn(wb[1], s_hi))
+    v_hi, v_lo = halves(rotated * scale)
+    v = nn(wc[0], v_hi) + (nn(wc[0], v_lo) + nn(wc[1], v_hi))
+    weights = mask_ref[pl.ds(pl.multiple_of(me * 32, 32), 32), :].astype(f32)
+    for gp in range(2):
+        y = jnp.concatenate(
+            [v[256 * p : 256 * p + 256, 128 * gp : 128 * gp + 128] for p in range(2)], axis=1
+        )
+        y_hi, y_lo = halves(y)
+        done = nt(y_hi, wa[0]) + (nt(y_lo, wa[0]) + nt(y_hi, wa[1]))
+        w16 = weights[16 * gp : 16 * gp + 16, :]
+        rows = pl.ds(pl.multiple_of(me * 32 + 16 * gp, 16), 16)
+        for j in range(32):
+            tile = jnp.concatenate(
+                [done[8 * j : 8 * j + 8, :128], done[8 * j : 8 * j + 8, 128:]], axis=0
+            )
+            gath[j // 8, rows, 128 * (j % 8) : 128 * (j % 8) + 128] = (tile * w16).astype(bf16)
+
+
+def kernel(
+    nz, q_ref, stored_ref, bi_ref, bo_ref, ev_ref, mask_ref, cnt_ref, out_ref,
+    st, gath, acc, sbuf, rbuf,
+    st_sem, recv_sem, up_sem, down_sem, y_sem, rs_send, rs_recv,
+):
+    layers = sbuf.shape[0]
+    width = st.shape[2]
+    me = lax.axis_index("doc")
+    mine = lax.axis_index("layer")
+    z, y = me // 2, me % 2
+    partner = me + 1 - 2 * y
+
+    def load(k):
+        return pltpu.make_async_copy(
+            stored_ref.at[0, :, pl.ds(k * width, width)], st.at[k], st_sem.at[k]
+        )
+
+    for k in range(N_CHUNK):
+        load(k).start()
+
+    barrier = pltpu.get_barrier_semaphore()
+    pl.semaphore_signal(barrier, inc=1, device_id={"doc": partner}, device_id_type=MESH)
+    for step in range(1, layers):
+        pl.semaphore_signal(
+            barrier, inc=1, device_id={"layer": lax.rem(mine + step, layers)}, device_id_type=MESH
+        )
+
+    @pl.when(z < nz - 1)
+    def _():
+        pl.semaphore_signal(barrier, inc=1, device_id={"doc": me + 2}, device_id_type=MESH)
+
+    @pl.when(z > 0)
+    def _():
+        pl.semaphore_signal(barrier, inc=1, device_id={"doc": me - 2}, device_id_type=MESH)
+
+    write_own_rows(q_ref, bi_ref, bo_ref, ev_ref, mask_ref, gath, me)
+
+    ends = jnp.where(z == 0, 1, 0) + jnp.where(z == nz - 1, 1, 0)
+    pl.semaphore_wait(barrier, layers + 2 - ends)
+
+    def plane_at(s):
+        far = (z >= 2).astype(jnp.int32)
+        near = z + far * (3 - 2 * z)
+        inner = (near == 1).astype(jnp.int32)
+        swap = inner * jnp.where(s < 2, 1, 0)
+        p = s + swap * (1 - 2 * s)
+        return p + far * (3 - 2 * p)
+
+    def send(p, side, k, sems, target):
+        blk = 2 * p + side
+        part = gath.at[k, pl.ds(pl.multiple_of(blk * 32, 32), 32)]
+        return pltpu.make_async_remote_copy(
+            src_ref=part, dst_ref=part, send_sem=sems.at[p, k], recv_sem=recv_sem.at[blk, k],
+            device_id={"doc": target}, device_id_type=MESH,
+        )
+
+    def forward(t):
+        p, k = plane_at(t // N_CHUNK), t % N_CHUNK
+
+        @pl.when(p != z)
+        def _():
+            send(p, y, k, y_sem, partner).wait_recv()
+
+        @pl.when((p <= z) & (z < nz - 1))
+        def _():
+            send(p, y, k, up_sem, me + 2).start()
+
+        @pl.when((p >= z) & (z > 0))
+        def _():
+            send(p, y, k, down_sem, me - 2).start()
+
+        send(p, y, k, y_sem, partner).start()
+
+    def hand_over(p, s):
+        return pltpu.make_async_remote_copy(
+            src_ref=sbuf.at[s], dst_ref=rbuf.at[mine], send_sem=rs_send.at[s],
+            recv_sem=rs_recv.at[mine], device_id={"layer": p}, device_id_type=MESH,
+        )
+
+    def compute(t):
+        s, k = t // N_CHUNK, t % N_CHUNK
+        p = plane_at(s)
+        send(p, 1 - y, k, y_sem, partner).wait_recv()
+
+        @pl.when(s == 0)
+        def _():
+            load(k).wait()
+
+        part = nt(gath[k, pl.ds(pl.multiple_of(p * 64, 64), 64), :], st[k])
+
+        @pl.when(k == 0)
+        def _():
+            acc[...] = part
+
+        @pl.when(k > 0)
+        def _():
+            acc[...] += part
+
+        @pl.when((k == N_CHUNK - 1) & (p == mine))
+        def _():
+            out_ref[...] = acc[...]
+
+        @pl.when((k == N_CHUNK - 1) & (p != mine))
+        def _():
+            sbuf[s] = acc[...].astype(bf16)
+            hand_over(p, s).start()
+
+    steps = nz * N_CHUNK
+
+    def first(t, carry):
+        forward(t)
+        return carry
+
+    def body(t, carry):
+        @pl.when(t + N_CHUNK < steps)
+        def _():
+            forward(t + N_CHUNK)
+
+        compute(t)
+        return carry
+
+    lax.fori_loop(0, N_CHUNK, first, 0)
+    lax.fori_loop(0, steps, body, 0)
+
+    def drain(t, carry):
+        p, k = t // N_CHUNK, t % N_CHUNK
+
+        @pl.when((p <= z) & (z < nz - 1))
+        def _():
+            send(p, y, k, up_sem, me + 2).wait_send()
+
+        @pl.when((p >= z) & (z > 0))
+        def _():
+            send(p, y, k, down_sem, me - 2).wait_send()
+
+        send(p, y, k, y_sem, partner).wait_send()
+        return carry
+
+    lax.fori_loop(0, steps, drain, 0)
+
+    total = out_ref[...]
+    for step in range(1, layers):
+        other = lax.rem(mine + step, layers)
+        pltpu.make_async_remote_copy(
+            src_ref=sbuf.at[0], dst_ref=rbuf.at[other], send_sem=rs_send.at[0],
+            recv_sem=rs_recv.at[other], device_id={"layer": other}, device_id_type=MESH,
+        ).wait_recv()
+        total = total + rbuf[other].astype(f32)
+    live = iota(total.shape, 1) < cnt_ref[0]
+    out_ref[...] = jnp.where(live, total, 0.0)
+    for s in range(nz):
+        p = plane_at(s)
+
+        @pl.when(p != mine)
+        def _():
+            hand_over(p, s).wait_send()
+
+
+def in_one_kernel(nz, query_grads, stored_grads, basis_in, basis_out, eigen_values, layer_mask, doc_counts):
+    layers = nz
+    _, docs, depth = stored_grads.shape
+    queries = layer_mask.shape[0]
+    rows = queries // layers
+    width = depth // N_CHUNK
+    vmem = pl.BlockSpec(memory_space=pltpu.VMEM)
+    return pl.pallas_call(
+        functools.partial(kernel, nz),
+        out_shape=jax.ShapeDtypeStruct((rows, docs), f32),
+        in_specs=[vmem, pl.BlockSpec(memory_space=pl.ANY), vmem, vmem, vmem, vmem,
+                  pl.BlockSpec(memory_space=pltpu.SMEM)],
+        out_specs=vmem,
+        scratch_shapes=[
+            pltpu.VMEM((N_CHUNK, docs, width), bf16),
+            pltpu.VMEM((N_CHUNK, queries, width), bf16),
+            pltpu.VMEM((rows, docs), f32),
+            pltpu.VMEM((layers, rows, docs), bf16),
+            pltpu.VMEM((layers, rows, docs), bf16),
+            pltpu.SemaphoreType.DMA((N_CHUNK,)),
+            pltpu.SemaphoreType.DMA((2 * nz, N_CHUNK)),
+            pltpu.SemaphoreType.DMA((nz, N_CHUNK)),
+            pltpu.SemaphoreType.DMA((nz, N_CHUNK)),
+            pltpu.SemaphoreType.DMA((nz, N_CHUNK)),
+            pltpu.SemaphoreType.DMA((layers,)),
+            pltpu.SemaphoreType.DMA((layers,)),
+        ],
+        compiler_params=pltpu.CompilerParams(
+            collective_id=0, has_side_effects=True, vmem_limit_bytes=58 * 1024 * 1024
+        ),
+        cost_estimate=pl.CostEstimate(
+            flops=2 * queries * docs * depth, bytes_accessed=2 * docs * depth, transcendentals=0
+        ),
+    )(query_grads, stored_grads, basis_in, basis_out, eigen_values, layer_mask, doc_counts)
+
+
+def on_device(query_grads, stored_grads, *rest):
+    n_doc, layers = lax.axis_size("doc"), lax.axis_size("layer")
+    shape = query_grads.shape
+    if n_doc == 8 and layers == 4 and shape == (1, 32, 4096):
+        return in_one_kernel(n_doc // 2, query_grads, stored_grads, *rest)
+    return by_collectives(query_grads, stored_grads, *rest)
 
 
 def solution(mesh):

time: 105 us -> 41.7 us (0.40); the launches traced: 103 us -> 40.9 us
  waiting for transfers between devices: 73.2 us -> 0 us
  Pallas kernels: 0 us -> 37.1 us
  between operations: 14.1 us -> 0.66 us
  matrix products: 11.9 us -> 0 us
    all_gather x1 -> x0, waiting for transfers between devices: 48.2 us -> none  [on_device(): lax.all_gather(own_rows, 'doc', axis=0, tiled=True) * row_weights[:, None]]
    pallas_call x0 -> x1, Pallas kernels: none -> 37.1 us  [in_one_kernel(): pl.pallas_call(functools.partial(kernel, nz), out_shape=jax.ShapeDtypeStr...]
    reduce_scatter x1 -> x0, waiting for transfers between devices: 25 us -> none  [on_device(): lax.psum_scatter(score_tiles, 'layer', scatter_dimension=0, tiled=True)]
    dot_general x5 -> x0, matrix products: 11.9 us -> none  [the longest x1 7.39 us: on_device(): lax.dot_general(masked, stored, (((1,), (1,)), ((), ())), preferred_eleme...]
    unnamed x6 -> x2, local copies, waits for them, and re-layouts: 0.01 us -> 3.14 us
    reshape x1 -> x0, local copies, waits for them, and re-layouts: 1.47 us -> none  [precondition(): gradients.astype(jnp.float32)]
    convert_element_type x1 -> x0, local copies, waits for them, and re-layouts: 1.17 us -> none  [precondition(): return restored.reshape(row_count, -1).astype(jnp.bfloat16)]
  transfers between devices with their start and end apart: 2 -> 0, of which waited for: 2 -> 0; matrix products, arithmetic and copies ran while one was open for 0% -> 0% of each run, Pallas kernels for 0% -> 0%
where the time goes in v1:
time: 41.7 us; the launch traced here: 40.9 us
  Pallas kernels  37.1 us (89%)
  local copies, waits for them, and re-layouts  3.14 us (8%)
  between operations  0.66 us (2%)
    pallas_call x1, Pallas kernels, in_one_kernel(): pl.pallas_call(functools.partial(kernel, nz), out_shape=jax.ShapeDtypeStr...  37.1 us
    unnamed x2, local copies, waits for them, and re-layouts  3.14 us

profile of v1, /device:TPU:24, one launch (start us, length us, event | category | flops | bytes accessed | tf_op | source)
XLA Modules:
  0.0 40.9 jit_solution(4497094397530570532)
XLA Ops:
  0.7 1.5 %copy.8.mask_ref = s32[256,1]{1,0:T(8,128)} copy(s32[256,1]{0,1:T(1,128)} %param.12) | data formatting | bytes 2048 | tf_op args[5]
  2.1 37.1 %shard_map.73 = f32[64,1024]{1,0:T(8,128)} custom-call(bf16[1,32,4096]{2,1,0:T(8,128)(2,1)} %q_ref.1, bf16[1,1024,4096]{2,1,0:T(8,128)(2,1)} %stored_ref.1, f32[1,64,64]{2,1,0:T(8,128)} %bi_ref.1, f32[1,64,64]{2,1,0:T(8,128)} %bo_ref.1, f32[1,64,64]{2,1,0:T(8,128)} %ev_ref.1, s32[256,1]{1,0:T(8,128)} %copy.8.mask_ref, s32[1]{0:T(128)S(6)} %copy.10.cnt_ref), custom_call_target="tpu_custom_call" | custom-call | flops 2147483648 | bytes 8388608 | tf_op jit(solution)/shard_map/pallas_call | solution.py:295
  39.2 1.7 %copy.11 = f32[64,1024]{1,0:T(8,128)} copy(f32[64,1024]{1,0:T(8,128)} %shard_map.73) | data formatting | bytes 524288

commit v2 on v1

--- a/solution.py
+++ b/solution.py
@@ -111,7 +111,8 @@
     rotated = nn(wb[0], s_hi) + (nn(wb[0], s_lo) + nn(wb[1], s_hi))
     v_hi, v_lo = halves(rotated * scale)
     v = nn(wc[0], v_hi) + (nn(wc[0], v_lo) + nn(wc[1], v_hi))
-    weights = mask_ref[pl.ds(pl.multiple_of(me * 32, 32), 32), :].astype(f32)
+    picked = iota((32, 256), 1) == me * 32 + iota((32, 256), 0)
+    weights = jnp.sum(jnp.where(picked, mask_ref[...].astype(f32), 0.0), axis=1, keepdims=True)
     for gp in range(2):
         y = jnp.concatenate(
             [v[256 * p : 256 * p + 256, 128 * gp : 128 * gp + 128] for p in range(2)], axis=1
@@ -128,12 +129,13 @@
 
 
 def kernel(
-    nz, q_ref, stored_ref, bi_ref, bo_ref, ev_ref, mask_ref, cnt_ref, out_ref,
+    nz, q_ref, stored_ref, bi_ref, bo_ref, ev_ref, mask_ref, out_ref,
     st, gath, acc, sbuf, rbuf,
     st_sem, recv_sem, up_sem, down_sem, y_sem, rs_send, rs_recv,
 ):
     layers = sbuf.shape[0]
     width = st.shape[2]
+    parts = sbuf.shape[1]
     me = lax.axis_index("doc")
     mine = lax.axis_index("layer")
     z, y = me // 2, me % 2
@@ -179,60 +181,123 @@
         blk = 2 * p + side
         part = gath.at[k, pl.ds(pl.multiple_of(blk * 32, 32), 32)]
         return pltpu.make_async_remote_copy(
-            src_ref=part, dst_ref=part, send_sem=sems.at[p, k], recv_sem=recv_sem.at[blk, k],
+            src_ref=part, dst_ref=part, send_sem=sems.at[blk, k], recv_sem=recv_sem.at[blk, k],
             device_id={"doc": target}, device_id_type=MESH,
         )
 
+    def up(p, side, k):
+        return send(p, side, k, up_sem, me + 2)
+
+    def down(p, side, k):
+        return send(p, side, k, down_sem, me - 2)
+
+    def across(p, k):
+        return send(p, y, k, y_sem, partner)
+
+    def landed(p, side, k):
+        return send(p, side, k, y_sem, partner)
+
+    def both_columns(p, k):
+        return ((p == 0) | (p == nz - 1)) & (k % 2 == 1)
+
+    def goes_up(p):
+        return (p <= z) & (z < nz - 1)
+
+    def goes_down(p):
+        return (p >= z) & (z > 0)
+
+    def goes_across(p, k):
+        return (p == z) | jnp.logical_not(both_columns(p, k))
+
+    def relayed(p, k):
+        return both_columns(p, k) & (p != z) & (p + z != nz - 1)
+
     def forward(t):
         p, k = plane_at(t // N_CHUNK), t % N_CHUNK
 
         @pl.when(p != z)
         def _():
-            send(p, y, k, y_sem, partner).wait_recv()
-
-        @pl.when((p <= z) & (z < nz - 1))
-        def _():
-            send(p, y, k, up_sem, me + 2).start()
-
-        @pl.when((p >= z) & (z > 0))
-        def _():
-            send(p, y, k, down_sem, me - 2).start()
-
-        send(p, y, k, y_sem, partner).start()
-
-    def hand_over(p, s):
+            landed(p, y, k).wait_recv()
+
+        @pl.when(goes_up(p))
+        def _():
+            up(p, y, k).start()
+
+        @pl.when(goes_down(p))
+        def _():
+            down(p, y, k).start()
+
+        @pl.when(goes_across(p, k))
+        def _():
+            across(p, k).start()
+
+    def pass_on(p, k):
+        @pl.when(goes_up(p))
+        def _():
+            up(p, 1 - y, k).start()
+
+        @pl.when(goes_down(p))
+        def _():
+            down(p, 1 - y, k).start()
+
+    def relay(t):
+        p, k = plane_at(t // N_CHUNK), t % N_CHUNK
+
+        @pl.when(relayed(p, k))
+        def _():
+            landed(p, 1 - y, k).wait_recv()
+            pass_on(p, k)
+
+    def hand_over(p, s, n):
         return pltpu.make_async_remote_copy(
-            src_ref=sbuf.at[s], dst_ref=rbuf.at[mine], send_sem=rs_send.at[s],
-            recv_sem=rs_recv.at[mine], device_id={"layer": p}, device_id_type=MESH,
+            src_ref=sbuf.at[s, n], dst_ref=rbuf.at[mine, n], send_sem=rs_send.at[s, n],
+            recv_sem=rs_recv.at[mine, n], device_id={"layer": p}, device_id_type=MESH,
         )
 
     def compute(t):
         s, k = t // N_CHUNK, t % N_CHUNK
         p = plane_at(s)
-        send(p, 1 - y, k, y_sem, partner).wait_recv()
+
+        @pl.when(jnp.logical_not(relayed(p, k)))
+        def _():
+            landed(p, 1 - y, k).wait_recv()
+
+        @pl.when((s == 0) & both_columns(p, k))
+        def _():
+            pass_on(p, k)
 
         @pl.when(s == 0)
         def _():
             load(k).wait()
 
-        part = nt(gath[k, pl.ds(pl.multiple_of(p * 64, 64), 64), :], st[k])
+        rows = pl.ds(pl.multiple_of(p * 64, 64), 64)
 
         @pl.when(k == 0)
         def _():
-            acc[...] = part
-
-        @pl.when(k > 0)
-        def _():
-            acc[...] += part
-
-        @pl.when((k == N_CHUNK - 1) & (p == mine))
-        def _():
-            out_ref[...] = acc[...]
-
-        @pl.when((k == N_CHUNK - 1) & (p != mine))
-        def _():
-            sbuf[s] = acc[...].astype(bf16)
-            hand_over(p, s).start()
+            acc[...] = nt(gath[k, rows, :], st[k])
+
+        @pl.when((k > 0) & (k < N_CHUNK - 1))
+        def _():
+            acc[...] += nt(gath[k, rows, :], st[k])
+
+        @pl.when(k == N_CHUNK - 1)
+        def _():
+            def column(n, carry):
+                cols = pl.ds(pl.multiple_of(n * 256, 256), 256)
+                total = acc[:, cols] + nt(gath[k, rows, :], st[k, cols, :])
+
+                @pl.when(p == mine)
+                def _():
+                    out_ref[:, cols] = total
+
+                @pl.when(p != mine)
+                def _():
+                    sbuf[s, n] = total.astype(bf16)
+                    hand_over(p, s, n).start()
+
+                return carry
+
+            lax.fori_loop(0, parts, column, 0)
 
     steps = nz * N_CHUNK
 
@@ -245,44 +310,69 @@
         def _():
             forward(t + N_CHUNK)
 
+        @pl.when(t + 1 < steps)
+        def _():
+            relay(t + 1)
+
         compute(t)
         return carry
 
     lax.fori_loop(0, N_CHUNK, first, 0)
     lax.fori_loop(0, steps, body, 0)
 
+    def collect(n, carry):
+        cols = pl.ds(pl.multiple_of(n * 256, 256), 256)
+        total = out_ref[:, cols]
+        for step in range(1, layers):
+            other = lax.rem(mine + step, layers)
+            pltpu.make_async_remote_copy(
+                src_ref=sbuf.at[0, n], dst_ref=rbuf.at[other, n], send_sem=rs_send.at[0, n],
+                recv_sem=rs_recv.at[other, n], device_id={"layer": other}, device_id_type=MESH,
+            ).wait_recv()
+            total = total + rbuf[other, n].astype(f32)
+        out_ref[:, cols] = total
+        return carry
+
+    lax.fori_loop(0, parts, collect, 0)
+
     def drain(t, carry):
         p, k = t // N_CHUNK, t % N_CHUNK
 
-        @pl.when((p <= z) & (z < nz - 1))
-        def _():
-            send(p, y, k, up_sem, me + 2).wait_send()
-
-        @pl.when((p >= z) & (z > 0))
-        def _():
-            send(p, y, k, down_sem, me - 2).wait_send()
-
-        send(p, y, k, y_sem, partner).wait_send()
+        @pl.when(goes_up(p))
+        def _():
+            up(p, y, k).wait_send()
+
+        @pl.when(goes_down(p))
+        def _():
+            down(p, y, k).wait_send()
+
+        @pl.when(both_columns(p, k) & goes_up(p))
+        def _():
+            up(p, 1 - y, k).wait_send()
+
+        @pl.when(both_columns(p, k) & goes_down(p))
+        def _():
+            down(p, 1 - y, k).wait_send()
+
+        @pl.when(goes_across(p, k))
+        def _():
+            across(p, k).wait_send()
+
         return carry
 
     lax.fori_loop(0, steps, drain, 0)
 
-    total = out_ref[...]
-    for step in range(1, layers):
-        other = lax.rem(mine + step, layers)
-        pltpu.make_async_remote_copy(
-            src_ref=sbuf.at[0], dst_ref=rbuf.at[other], send_sem=rs_send.at[0],
-            recv_sem=rs_recv.at[other], device_id={"layer": other}, device_id_type=MESH,
-        ).wait_recv()
-        total = total + rbuf[other].astype(f32)
-    live = iota(total.shape, 1) < cnt_ref[0]
-    out_ref[...] = jnp.where(live, total, 0.0)
-    for s in range(nz):
+    def drain_scores(t, carry):
+        s, n = t // parts, t % parts
         p = plane_at(s)
 
         @pl.when(p != mine)
         def _():
-            hand_over(p, s).wait_send()
+            hand_over(p, s, n).wait_send()
+
+        return carry
+
+    lax.fori_loop(0, nz * parts, drain_scores, 0)
 
 
 def in_one_kernel(nz, query_grads, stored_grads, basis_in, basis_out, eigen_values, layer_mask, doc_counts):
@@ -292,25 +382,24 @@
     rows = queries // layers
     width = depth // N_CHUNK
     vmem = pl.BlockSpec(memory_space=pltpu.VMEM)
-    return pl.pallas_call(
+    summed = pl.pallas_call(
         functools.partial(kernel, nz),
         out_shape=jax.ShapeDtypeStruct((rows, docs), f32),
-        in_specs=[vmem, pl.BlockSpec(memory_space=pl.ANY), vmem, vmem, vmem, vmem,
-                  pl.BlockSpec(memory_space=pltpu.SMEM)],
+        in_specs=[vmem, pl.BlockSpec(memory_space=pl.ANY), vmem, vmem, vmem, vmem],
         out_specs=vmem,
         scratch_shapes=[
             pltpu.VMEM((N_CHUNK, docs, width), bf16),
             pltpu.VMEM((N_CHUNK, queries, width), bf16),
             pltpu.VMEM((rows, docs), f32),
-            pltpu.VMEM((layers, rows, docs), bf16),
-            pltpu.VMEM((layers, rows, docs), bf16),
+            pltpu.VMEM((nz, docs // 256, rows, 256), bf16),
+            pltpu.VMEM((layers, docs // 256, rows, 256), bf16),
             pltpu.SemaphoreType.DMA((N_CHUNK,)),
             pltpu.SemaphoreType.DMA((2 * nz, N_CHUNK)),
-            pltpu.SemaphoreType.DMA((nz, N_CHUNK)),
-            pltpu.SemaphoreType.DMA((nz, N_CHUNK)),
-            pltpu.SemaphoreType.DMA((nz, N_CHUNK)),
-            pltpu.SemaphoreType.DMA((layers,)),
-            pltpu.SemaphoreType.DMA((layers,)),
+            pltpu.SemaphoreType.DMA((2 * nz, N_CHUNK)),
+            pltpu.SemaphoreType.DMA((2 * nz, N_CHUNK)),
+            pltpu.SemaphoreType.DMA((2 * nz, N_CHUNK)),
+            pltpu.SemaphoreType.DMA((nz, docs // 256)),
+            pltpu.SemaphoreType.DMA((layers, docs // 256)),
         ],
         compiler_params=pltpu.CompilerParams(
             collective_id=0, has_side_effects=True, vmem_limit_bytes=58 * 1024 * 1024
@@ -318,7 +407,9 @@
         cost_estimate=pl.CostEstimate(
             flops=2 * queries * docs * depth, bytes_accessed=2 * docs * depth, transcendentals=0
         ),
-    )(query_grads, stored_grads, basis_in, basis_out, eigen_values, layer_mask, doc_counts)
+    )(query_grads, stored_grads, basis_in, basis_out, eigen_values, layer_mask.reshape(1, queries))
+    live_slots = jnp.arange(docs, dtype=jnp.int32) < doc_counts[0]
+    return jnp.where(live_slots[None, :], summed, jnp.zeros_like(summed))
 
 
 def on_device(query_grads, stored_grads, *rest):

time: 41.7 us -> 41.9 us (level); the launches traced: 40.9 us -> 41.6 us
  local copies, waits for them, and re-layouts: 3.14 us -> 0 us
  Pallas kernels: 37.1 us -> 39.2 us
  other arithmetic: 0 us -> 1.68 us
    unnamed x2 -> x0, local copies, waits for them, and re-layouts: 3.14 us -> none
    pallas_call x1, Pallas kernels: 37.1 us -> 39.2 us  [in_one_kernel(): pl.pallas_call(functools.partial(kernel, nz), out_shape=jax.ShapeDtypeStr...]
    select_n x0 -> x1, other arithmetic: none -> 1.67 us  [in_one_kernel(): return jnp.where(live_slots[None, :], summed, jnp.zeros_like(summed))]
where the time goes in v2:
time: 41.9 us; the launch traced here: 41.6 us
  Pallas kernels  39.2 us (94%)
  other arithmetic  1.68 us (4%)
  between operations  0.67 us (2%)
    pallas_call x1, Pallas kernels, in_one_kernel(): pl.pallas_call(functools.partial(kernel, nz), out_shape=jax.ShapeDtypeStr...  39.2 us
    select_n x1, other arithmetic, in_one_kernel(): return jnp.where(live_slots[None, :], summed, jnp.zeros_like(summed))  1.67 us

profile of v2, /device:TPU:24, one launch (start us, length us, event | category | flops | bytes accessed | tf_op | source)
XLA Modules:
  0.0 41.6 jit_solution(2042180270827246170)
XLA Ops:
  0.7 39.2 %shard_map.73 = f32[64,1024]{1,0:T(8,128)} custom-call(bf16[1,32,4096]{2,1,0:T(8,128)(2,1)} %q_ref.1, bf16[1,1024,4096]{2,1,0:T(8,128)(2,1)} %stored_ref.1, f32[1,64,64]{2,1,0:T(8,128)} %bi_ref.1, f32[1,64,64]{2,1,0:T(8,128)} %bo_ref.1, f32[1,64,64]{2,1,0:T(8,128)} %ev_ref.1, s32[1,256]{1,0:T(1,128)} %bitcast.3), custom_call_target="tpu_custom_call" | custom-call | flops 2147483648 | bytes 8388608 | tf_op jit(solution)/shard_map/pallas_call | solution.py:385
  39.9 1.7 %broadcast_select_fusion = f32[64,1024]{1,0:T(8,128)} fusion(f32[64,1024]{1,0:T(8,128)} %shard_map.73, pred[1024]{0:T(1024)(128)(4,1)S(1)} %iota_compare_fusion), kind=kLoop, calls=%fused_computation | loop fusion | flops 65536 | bytes 525312 | tf_op jit(solution)/shard_map/jit(_where)/select_n | solution.py:412
  (1 shorter events, 0.0 us)

commit v3 on v2

--- a/solution.py
+++ b/solution.py
@@ -54,6 +54,12 @@
     return lax.dot_general(a, b, (((1,), (1,)), ((), ())), preferred_element_type=f32)
 
 
+def three(a, b_hi, b_lo):
+    both = nn(a[0], jnp.concatenate([b_hi, b_lo], axis=1))
+    width = b_hi.shape[1]
+    return both[:, :width] + (both[:, width:] + nn(a[1], b_hi))
+
+
 def one_hot(hits):
     return jnp.where(hits, 1.0, 0.0).astype(bf16)
 
@@ -62,8 +68,7 @@
     return lax.broadcasted_iota(jnp.int32, shape, dim)
 
 
-def write_own_rows(q_ref, bi_ref, bo_ref, ev_ref, mask_ref, gath, me):
-    x = q_ref[0].astype(f32)
+def write_own_rows(q_ref, bi_ref, bo_ref, ev_ref, mask_ref, gath, me, ready, send_rows):
     r, c = iota((256, 256), 0), iota((256, 256), 1)
     same = (r // 128 == (c // 64) % 2) & ((r // 64) % 2 == c // 128)
     put_a = one_hot(iota((256, 64), 0) % 64 == iota((256, 64), 1))
@@ -84,48 +89,42 @@
     mid, low = halves(low)
     scale = 0.0
     for part in (top, mid, low):
-        scale = scale + nt(nn(put_b, part).astype(bf16), put_a)
-
-    turned = []
-    for gp in range(2):
-        pieces = [
-            jnp.concatenate(
-                [
-                    x[8 * (2 * gp + g) : 8 * (2 * gp + g) + 8, 128 * j : 128 * j + 128]
-                    for j in range(32)
-                ],
-                axis=0,
-            )
-            for g in range(2)
-        ]
-        block = jnp.concatenate(pieces, axis=1).astype(bf16)
-        turned.append(nn(block, wa[0]) + nn(block, wa[1]))
-    s = jnp.concatenate(
-        [
-            jnp.concatenate([turned[gp][:, 128 * p : 128 * p + 128] for gp in range(2)], axis=1)
-            for p in range(2)
-        ],
-        axis=0,
-    )
-    s_hi, s_lo = halves(s)
-    rotated = nn(wb[0], s_hi) + (nn(wb[0], s_lo) + nn(wb[1], s_hi))
-    v_hi, v_lo = halves(rotated * scale)
-    v = nn(wc[0], v_hi) + (nn(wc[0], v_lo) + nn(wc[1], v_hi))
-    picked = iota((32, 256), 1) == me * 32 + iota((32, 256), 0)
-    weights = jnp.sum(jnp.where(picked, mask_ref[...].astype(f32), 0.0), axis=1, keepdims=True)
-    for gp in range(2):
-        y = jnp.concatenate(
-            [v[256 * p : 256 * p + 256, 128 * gp : 128 * gp + 128] for p in range(2)], axis=1
-        )
-        y_hi, y_lo = halves(y)
+        scale = scale + nt(nn(put_b, part).astype(bf16), put_a[:128])
+    ready()
+
+
+    def rows_of_16(gp, carry):
+        x = q_ref[0, pl.ds(pl.multiple_of(16 * gp, 16), 16), :].astype(f32)
+        block = jnp.concatenate(
+            [
+                jnp.concatenate(
+                    [x[8 * g : 8 * g + 8, 128 * j : 128 * j + 128] for j in range(32)], axis=0
+                )
+                for g in range(2)
+            ],
+            axis=1,
+        ).astype(bf16)
+        turned = nn(block, wa[0]) + nn(block, wa[1])
+        s = jnp.concatenate([turned[:, :128], turned[:, 128:]], axis=0)
+        s_hi, s_lo = halves(s)
+        rotated = three(wb, s_hi, s_lo)
+        v_hi, v_lo = halves(rotated * scale)
+        v = three(wc, v_hi, v_lo)
+        y_hi, y_lo = halves(jnp.concatenate([v[:256], v[256:]], axis=1))
         done = nt(y_hi, wa[0]) + (nt(y_lo, wa[0]) + nt(y_hi, wa[1]))
-        w16 = weights[16 * gp : 16 * gp + 16, :]
-        rows = pl.ds(pl.multiple_of(me * 32 + 16 * gp, 16), 16)
+        start = me * 32 + 16 * gp
+        picked = iota((16, 256), 1) == start + iota((16, 256), 0)
+        w16 = jnp.sum(jnp.where(picked, mask_ref[...].astype(f32), 0.0), axis=1, keepdims=True)
+        rows = pl.ds(pl.multiple_of(start, 16), 16)
         for j in range(32):
             tile = jnp.concatenate(
                 [done[8 * j : 8 * j + 8, :128], done[8 * j : 8 * j + 8, 128:]], axis=0
             )
             gath[j // 8, rows, 128 * (j % 8) : 128 * (j % 8) + 128] = (tile * w16).astype(bf16)
+        send_rows(gp)
+        return carry
+
+    lax.fori_loop(0, 2, rows_of_16, 0)
 
 
 def kernel(
@@ -164,11 +163,6 @@
     def _():
         pl.semaphore_signal(barrier, inc=1, device_id={"doc": me - 2}, device_id_type=MESH)
 
-    write_own_rows(q_ref, bi_ref, bo_ref, ev_ref, mask_ref, gath, me)
-
-    ends = jnp.where(z == 0, 1, 0) + jnp.where(z == nz - 1, 1, 0)
-    pl.semaphore_wait(barrier, layers + 2 - ends)
-
     def plane_at(s):
         far = (z >= 2).astype(jnp.int32)
         near = z + far * (3 - 2 * z)
@@ -177,22 +171,25 @@
         p = s + swap * (1 - 2 * s)
         return p + far * (3 - 2 * p)
 
-    def send(p, side, k, sems, target):
+    def send(p, side, k, sems, target, gp=None):
         blk = 2 * p + side
-        part = gath.at[k, pl.ds(pl.multiple_of(blk * 32, 32), 32)]
+        if gp is None:
+            part = gath.at[k, pl.ds(pl.multiple_of(blk * 32, 32), 32)]
+        else:
+            part = gath.at[k, pl.ds(pl.multiple_of(blk * 32 + gp * 16, 16), 16)]
         return pltpu.make_async_remote_copy(
             src_ref=part, dst_ref=part, send_sem=sems.at[blk, k], recv_sem=recv_sem.at[blk, k],
             device_id={"doc": target}, device_id_type=MESH,
         )
 
-    def up(p, side, k):
-        return send(p, side, k, up_sem, me + 2)
-
-    def down(p, side, k):
-        return send(p, side, k, down_sem, me - 2)
-
-    def across(p, k):
-        return send(p, y, k, y_sem, partner)
+    def up(p, side, k, gp=None):
+        return send(p, side, k, up_sem, me + 2, gp)
+
+    def down(p, side, k, gp=None):
+        return send(p, side, k, down_sem, me - 2, gp)
+
+    def across(p, k, gp=None):
+        return send(p, y, k, y_sem, partner, gp)
 
     def landed(p, side, k):
         return send(p, side, k, y_sem, partner)
@@ -215,9 +212,7 @@
     def forward(t):
         p, k = plane_at(t // N_CHUNK), t % N_CHUNK
 
-        @pl.when(p != z)
-        def _():
-            landed(p, y, k).wait_recv()
+        landed(p, y, k).wait_recv()
 
         @pl.when(goes_up(p))
         def _():
@@ -227,9 +222,28 @@
         def _():
             down(p, y, k).start()
 
-        @pl.when(goes_across(p, k))
+        @pl.when(jnp.logical_not(both_columns(p, k)))
         def _():
             across(p, k).start()
+
+    def send_rows(gp):
+        def chunk(k, carry):
+            @pl.when(z < nz - 1)
+            def _():
+                up(z, y, k, gp).start()
+
+            @pl.when(z > 0)
+            def _():
+                down(z, y, k, gp).start()
+
+            across(z, k, gp).start()
+            return carry
+
+        lax.fori_loop(0, N_CHUNK, chunk, 0)
+
+    def ready():
+        ends = jnp.where(z == 0, 1, 0) + jnp.where(z == nz - 1, 1, 0)
+        pl.semaphore_wait(barrier, layers + 2 - ends)
 
     def pass_on(p, k):
         @pl.when(goes_up(p))
@@ -274,9 +288,9 @@
 
         @pl.when(k == 0)
         def _():
-            acc[...] = nt(gath[k, rows, :], st[k])
-
-        @pl.when((k > 0) & (k < N_CHUNK - 1))
+            acc[...] = jnp.zeros_like(acc)
+
+        @pl.when(k < N_CHUNK - 1)
         def _():
             acc[...] += nt(gath[k, rows, :], st[k])
 
@@ -306,18 +320,20 @@
         return carry
 
     def body(t, carry):
-        @pl.when(t + N_CHUNK < steps)
-        def _():
-            forward(t + N_CHUNK)
-
-        @pl.when(t + 1 < steps)
-        def _():
-            relay(t + 1)
+        @pl.when(t + lead < steps)
+        def _():
+            forward(t + lead)
+
+        @pl.when(t + 2 < steps)
+        def _():
+            relay(t + 2)
 
         compute(t)
         return carry
 
-    lax.fori_loop(0, N_CHUNK, first, 0)
+    write_own_rows(q_ref, bi_ref, bo_ref, ev_ref, mask_ref, gath, me, ready, send_rows)
+    lead = N_CHUNK * jnp.where((z == 0) | (z == nz - 1), 1, 2)
+    lax.fori_loop(N_CHUNK, lead, first, 0)
     lax.fori_loop(0, steps, body, 0)
 
     def collect(n, carry):
@@ -385,7 +401,7 @@
     summed = pl.pallas_call(
         functools.partial(kernel, nz),
         out_shape=jax.ShapeDtypeStruct((rows, docs), f32),
-        in_specs=[vmem, pl.BlockSpec(memory_space=pl.ANY), vmem, vmem, vmem, vmem],
+        in_specs=[vmem, pl.BlockSpec(memory_space=pltpu.HBM), vmem, vmem, vmem, vmem],
         out_specs=vmem,
         scratch_shapes=[
             pltpu.VMEM((N_CHUNK, docs, width), bf16),
@@ -402,7 +418,7 @@
             pltpu.SemaphoreType.DMA((layers, docs // 256)),
         ],
         compiler_params=pltpu.CompilerParams(
-            collective_id=0, has_side_effects=True, vmem_limit_bytes=58 * 1024 * 1024
+            collective_id=0, has_side_effects=True, vmem_limit_bytes=50 * 1024 * 1024
         ),
         cost_estimate=pl.CostEstimate(
             flops=2 * queries * docs * depth, bytes_accessed=2 * docs * depth, transcendentals=0

time: 41.9 us -> 40.4 us (0.964)
  Pallas kernels: 39.2 us -> 34.6 us
  local copies, waits for them, and re-layouts: 0 us -> 3.9 us
  other arithmetic: 1.68 us -> 0.73 us
    pallas_call x1, Pallas kernels: 39.2 us -> 34.6 us  [in_one_kernel(): pl.pallas_call(functools.partial(kernel, nz), out_shape=jax.ShapeDtypeStr...]
    unnamed x0 -> x10, local copies, waits for them, and re-layouts: none -> 3.9 us
    select_n x1, other arithmetic: 1.67 us -> 0.73 us  [in_one_kernel(): return jnp.where(live_slots[None, :], summed, jnp.zeros_like(summed))]
where the time goes in v3:
time: 40.4 us; the launch traced here: 39.9 us
  Pallas kernels  34.6 us (86%)
  local copies, waits for them, and re-layouts  3.9 us (10%)
  other arithmetic  0.73 us (2%)
  between operations  0.68 us (2%)
    pallas_call x1, Pallas kernels, in_one_kernel(): pl.pallas_call(functools.partial(kernel, nz), out_shape=jax.ShapeDtypeStr...  34.6 us
    unnamed x10, local copies, waits for them, and re-layouts  3.9 us

profile of v3, /device:TPU:24, one launch (start us, length us, event | category | flops | bytes accessed | tf_op | source)
XLA Modules:
  0.0 39.9 jit_solution(7418723868539580860)
XLA Ops:
  0.7 0.0 copy-start
  0.7 0.9 %copy-done = bf16[1,32,4096]{2,1,0:T(8,128)(2,1)S(1)} copy-done((bf16[1,32,4096]{2,1,0:T(8,128)(2,1)S(1)}, bf16[1,32,4096]{2,1,0:T(8,128)(2,1)}, u32[]{:S(2)}) %copy-start) | copy-done | bytes 262168
  1.6 0.0 copy-start.1
  1.6 0.8 %copy-done.1 = f32[1,64,64]{2,1,0:T(8,128)S(1)} copy-done((f32[1,64,64]{2,1,0:T(8,128)S(1)}, f32[1,64,64]{2,1,0:T(8,128)}, u32[]{:S(2)}) %copy-start.1) | copy-done | bytes 16408
  2.4 0.0 copy-start.2
  2.4 0.8 %copy-done.2 = f32[1,64,64]{2,1,0:T(8,128)S(1)} copy-done((f32[1,64,64]{2,1,0:T(8,128)S(1)}, f32[1,64,64]{2,1,0:T(8,128)}, u32[]{:S(2)}) %copy-start.2) | copy-done | bytes 16408
  3.1 0.0 copy-start.3
  3.1 0.8 %copy-done.3 = f32[1,64,64]{2,1,0:T(8,128)S(1)} copy-done((f32[1,64,64]{2,1,0:T(8,128)S(1)}, f32[1,64,64]{2,1,0:T(8,128)}, u32[]{:S(2)}) %copy-start.3) | copy-done | bytes 16408
  3.9 0.0 copy-start.4
  3.9 0.7 %copy-done.4 = s32[256,1]{0,1:T(1,128)S(1)} copy-done((s32[256,1]{0,1:T(1,128)S(1)}, s32[256,1]{0,1:T(1,128)}, u32[]{:S(2)}) %copy-start.4) | copy-done | bytes 1048
  4.6 34.6 %shard_map.73 = f32[64,1024]{1,0:T(8,128)S(1)} custom-call(bf16[1,32,4096]{2,1,0:T(8,128)(2,1)S(1)} %copy-done, bf16[1,1024,4096]{2,1,0:T(8,128)(2,1)} %stored_ref.1, f32[1,64,64]{2,1,0:T(8,128)S(1)} %copy-done.1, f32[1,64,64]{2,1,0:T(8,128)S(1)} %copy-done.2, f32[1,64,64]{2,1,0:T(8,128)S(1)} %copy-done.3, s32[1,256]{1,0:T(1,128)S(1)} %bitcast.3), custom_call_target="tpu_custom_call" | custom-call | flops 2147483648 | bytes 8388608 | tf_op jit(solution)/shard_map/pallas_call | solution.py:401
  39.2 0.7 %broadcast_select_fusion = f32[64,1024]{1,0:T(8,128)} fusion(f32[64,1024]{1,0:T(8,128)S(1)} %shard_map.73, pred[1024]{0:T(1024)(128)(4,1)S(1)} %iota_compare_fusion), kind=kLoop, calls=%fused_computation | loop fusion | flops 65536 | bytes 525312 | tf_op jit(solution)/shard_map/jit(_where)/select_n | solution.py:428
  (1 shorter events, 0.0 us)
Async XLA Ops:
  0.7 1.0 %copy-start = (bf16[1,32,4096]{2,1,0:T(8,128)(2,1)S(1)}, bf16[1,32,4096]{2,1,0:T(8,128)(2,1)}, u32[]{:S(2)}) copy-start(bf16[1,32,4096]{2,1,0:T(8,128)(2,1)} %q_ref.1) | copy-start | bytes 786436
  1.6 0.8 %copy-start.1 = (f32[1,64,64]{2,1,0:T(8,128)S(1)}, f32[1,64,64]{2,1,0:T(8,128)}, u32[]{:S(2)}) copy-start(f32[1,64,64]{2,1,0:T(8,128)} %bi_ref.1) | copy-start | bytes 49156
  2.4 0.8 %copy-start.2 = (f32[1,64,64]{2,1,0:T(8,128)S(1)}, f32[1,64,64]{2,1,0:T(8,128)}, u32[]{:S(2)}) copy-start(f32[1,64,64]{2,1,0:T(8,128)} %bo_ref.1) | copy-start | bytes 49156
  3.1 0.8 %copy-start.3 = (f32[1,64,64]{2,1,0:T(8,128)S(1)}, f32[1,64,64]{2,1,0:T(8,128)}, u32[]{:S(2)}) copy-start(f32[1,64,64]{2,1,0:T(8,128)} %ev_ref.1) | copy-start | bytes 49156
  3.9 0.7 %copy-start.4 = (s32[256,1]{0,1:T(1,128)S(1)}, s32[256,1]{0,1:T(1,128)}, u32[]{:S(2)}) copy-start(s32[256,1]{0,1:T(1,128)} %param.12) | copy-start | bytes 3076

commit v4 on v2

--- a/solution.py
+++ b/solution.py
@@ -62,8 +62,14 @@
     return lax.broadcasted_iota(jnp.int32, shape, dim)
 
 
-def write_own_rows(q_ref, bi_ref, bo_ref, ev_ref, mask_ref, gath, me):
-    x = q_ref[0].astype(f32)
+def stacked(x):
+    hi, lo = halves(x)
+    return jnp.concatenate([hi, lo, hi], axis=0)
+
+
+def write_own_rows(q_ref, bi_ref, bo_ref, ev_ref, mask_ref, xs, gath, me, ready, send_rows):
+    for j in range(32):
+        xs[32 * j : 32 * j + 32, :] = q_ref[0, :, 128 * j : 128 * j + 128].astype(f32)
     r, c = iota((256, 256), 0), iota((256, 256), 1)
     same = (r // 128 == (c // 64) % 2) & ((r // 64) % 2 == c // 128)
     put_a = one_hot(iota((256, 64), 0) % 64 == iota((256, 64), 1))
@@ -71,66 +77,78 @@
         jnp.where(same, nt(nn(put_a, part).astype(bf16), put_a), 0.0).astype(bf16)
         for part in halves(bi_ref[0])
     ]
-    row = iota((512, 64), 0)
-    put_b = one_hot(2 * ((row // 8) % 32) + row // 256 == iota((512, 64), 1))
-    eye = iota((512, 512), 0) % 8 == iota((512, 512), 1) % 8
-    wc, wb = [], []
-    for part in halves(bo_ref[0]):
-        wc.append(jnp.where(eye, nt(nn(put_b, part).astype(bf16), put_b), 0.0).astype(bf16))
-        wb.append(jnp.where(eye, nt(nt(put_b, part).astype(bf16), put_b), 0.0).astype(bf16))
+    row = iota((64, 64), 0)
+    put_b = one_hot(2 * (row % 32) + row // 32 == iota((64, 64), 1))
+    col = iota((192, 64), 0)
+    order = 2 * (col % 32) + (col // 32) % 2 == iota((192, 64), 1)
+    place = [one_hot(order & (col < 128)), one_hot(order & (col >= 128))]
+    wb, wc = 0.0, 0.0
+    for part, to in zip(halves(bo_ref[0]), place):
+        wb = wb + nt(nt(put_b, part).astype(bf16), to)
+        wc = wc + nt(nn(put_b, part).astype(bf16), to)
+    wb, wc = wb.astype(bf16), wc.astype(bf16)
     inverse = 1.0 / (ev_ref[0] + damping)
-    top, low = halves(inverse)
-    low = inverse - top.astype(f32)
-    mid, low = halves(low)
+    top = inverse.astype(bf16)
     scale = 0.0
-    for part in (top, mid, low):
-        scale = scale + nt(nn(put_b, part).astype(bf16), put_a)
-
-    turned = []
-    for gp in range(2):
-        pieces = [
+    for part in (top,) + halves(inverse - top.astype(f32)):
+        scale = scale + nt(nn(put_b, part).astype(bf16), put_a[:128])
+    scale = jnp.concatenate([scale] * 16, axis=1)
+
+    block = jnp.concatenate(
+        [
             jnp.concatenate(
-                [
-                    x[8 * (2 * gp + g) : 8 * (2 * gp + g) + 8, 128 * j : 128 * j + 128]
-                    for j in range(32)
-                ],
-                axis=0,
+                [xs[pl.ds(q + 16 * g, 32, stride=32), :] for g in range(2)], axis=1
             )
-            for g in range(2)
-        ]
-        block = jnp.concatenate(pieces, axis=1).astype(bf16)
-        turned.append(nn(block, wa[0]) + nn(block, wa[1]))
+            for q in range(16)
+        ],
+        axis=0,
+    ).astype(bf16)
+    turned = nn(block, wa[0]) + nn(block, wa[1])
     s = jnp.concatenate(
         [
-            jnp.concatenate([turned[gp][:, 128 * p : 128 * p + 128] for gp in range(2)], axis=1)
-            for p in range(2)
+            jnp.concatenate(
+                [turned[32 * q : 32 * q + 32, 128 * p : 128 * p + 128] for p in range(2)], axis=0
+            )
+            for q in range(16)
+        ],
+        axis=1,
+    )
+    rotated = nn(wb, stacked(s))
+    v = nn(wc, stacked(rotated * scale))
+    y = jnp.concatenate(
+        [
+            jnp.concatenate(
+                [v[32 * p : 32 * p + 32, 128 * q : 128 * q + 128] for p in range(2)], axis=1
+            )
+            for q in range(16)
         ],
         axis=0,
     )
-    s_hi, s_lo = halves(s)
-    rotated = nn(wb[0], s_hi) + (nn(wb[0], s_lo) + nn(wb[1], s_hi))
-    v_hi, v_lo = halves(rotated * scale)
-    v = nn(wc[0], v_hi) + (nn(wc[0], v_lo) + nn(wc[1], v_hi))
+    y_hi, y_lo = halves(y)
+    done = nt(y_hi, wa[0]) + (nt(y_lo, wa[0]) + nt(y_hi, wa[1]))
+    for q in range(16):
+        for g in range(2):
+            xs[pl.ds(q + 16 * g, 32, stride=32), :] = done[
+                32 * q : 32 * q + 32, 128 * g : 128 * g + 128
+            ]
     picked = iota((32, 256), 1) == me * 32 + iota((32, 256), 0)
     weights = jnp.sum(jnp.where(picked, mask_ref[...].astype(f32), 0.0), axis=1, keepdims=True)
-    for gp in range(2):
-        y = jnp.concatenate(
-            [v[256 * p : 256 * p + 256, 128 * gp : 128 * gp + 128] for p in range(2)], axis=1
-        )
-        y_hi, y_lo = halves(y)
-        done = nt(y_hi, wa[0]) + (nt(y_lo, wa[0]) + nt(y_hi, wa[1]))
-        w16 = weights[16 * gp : 16 * gp + 16, :]
-        rows = pl.ds(pl.multiple_of(me * 32 + 16 * gp, 16), 16)
-        for j in range(32):
-            tile = jnp.concatenate(
-                [done[8 * j : 8 * j + 8, :128], done[8 * j : 8 * j + 8, 128:]], axis=0
-            )
-            gath[j // 8, rows, 128 * (j % 8) : 128 * (j % 8) + 128] = (tile * w16).astype(bf16)
+    rows = pl.ds(pl.multiple_of(me * 32, 32), 32)
+    ready()
+
+    def chunk(k, carry):
+        for j in range(8):
+            tile = xs[pl.ds(pl.multiple_of(256 * k + 32 * j, 32), 32), :]
+            gath[k, rows, 128 * j : 128 * j + 128] = (tile * weights).astype(bf16)
+        send_rows(k)
+        return carry
+
+    lax.fori_loop(0, N_CHUNK, chunk, 0)
 
 
 def kernel(
     nz, q_ref, stored_ref, bi_ref, bo_ref, ev_ref, mask_ref, out_ref,
-    st, gath, acc, sbuf, rbuf,
+    xs, st, gath, acc, sbuf, rbuf,
     st_sem, recv_sem, up_sem, down_sem, y_sem, rs_send, rs_recv,
 ):
     layers = sbuf.shape[0]
@@ -164,11 +182,6 @@
     def _():
         pl.semaphore_signal(barrier, inc=1, device_id={"doc": me - 2}, device_id_type=MESH)
 
-    write_own_rows(q_ref, bi_ref, bo_ref, ev_ref, mask_ref, gath, me)
-
-    ends = jnp.where(z == 0, 1, 0) + jnp.where(z == nz - 1, 1, 0)
-    pl.semaphore_wait(barrier, layers + 2 - ends)
-
     def plane_at(s):
         far = (z >= 2).astype(jnp.int32)
         near = z + far * (3 - 2 * z)
@@ -215,9 +228,7 @@
     def forward(t):
         p, k = plane_at(t // N_CHUNK), t % N_CHUNK
 
-        @pl.when(p != z)
-        def _():
-            landed(p, y, k).wait_recv()
+        landed(p, y, k).wait_recv()
 
         @pl.when(goes_up(p))
         def _():
@@ -227,9 +238,24 @@
         def _():
             down(p, y, k).start()
 
-        @pl.when(goes_across(p, k))
+        @pl.when(jnp.logical_not(both_columns(p, k)))
         def _():
             across(p, k).start()
+
+    def send_rows(k):
+        @pl.when(z < nz - 1)
+        def _():
+            up(z, y, k).start()
+
+        @pl.when(z > 0)
+        def _():
+            down(z, y, k).start()
+
+        across(z, k).start()
+
+    def ready():
+        ends = jnp.where(z == 0, 1, 0) + jnp.where(z == nz - 1, 1, 0)
+        pl.semaphore_wait(barrier, layers + 2 - ends)
 
     def pass_on(p, k):
         @pl.when(goes_up(p))
@@ -274,9 +300,9 @@
 
         @pl.when(k == 0)
         def _():
-            acc[...] = nt(gath[k, rows, :], st[k])
-
-        @pl.when((k > 0) & (k < N_CHUNK - 1))
+            acc[...] = jnp.zeros_like(acc)
+
+        @pl.when(k < N_CHUNK - 1)
         def _():
             acc[...] += nt(gath[k, rows, :], st[k])
 
@@ -306,18 +332,20 @@
         return carry
 
     def body(t, carry):
-        @pl.when(t + N_CHUNK < steps)
-        def _():
-            forward(t + N_CHUNK)
-
-        @pl.when(t + 1 < steps)
-        def _():
-            relay(t + 1)
+        @pl.when(t + lead < steps)
+        def _():
+            forward(t + lead)
+
+        @pl.when(t + 2 < steps)
+        def _():
+            relay(t + 2)
 
         compute(t)
         return carry
 
-    lax.fori_loop(0, N_CHUNK, first, 0)
+    write_own_rows(q_ref, bi_ref, bo_ref, ev_ref, mask_ref, xs, gath, me, ready, send_rows)
+    lead = N_CHUNK * jnp.where((z == 0) | (z == nz - 1), 1, 2)
+    lax.fori_loop(N_CHUNK, lead, first, 0)
     lax.fori_loop(0, steps, body, 0)
 
     def collect(n, carry):
@@ -385,9 +413,10 @@
     summed = pl.pallas_call(
         functools.partial(kernel, nz),
         out_shape=jax.ShapeDtypeStruct((rows, docs), f32),
-        in_specs=[vmem, pl.BlockSpec(memory_space=pl.ANY), vmem, vmem, vmem, vmem],
+        in_specs=[vmem, pl.BlockSpec(memory_space=pltpu.HBM), vmem, vmem, vmem, vmem],
         out_specs=vmem,
         scratch_shapes=[
+            pltpu.VMEM((depth * query_grads.shape[1] // 128, 128), f32),
             pltpu.VMEM((N_CHUNK, docs, width), bf16),
             pltpu.VMEM((N_CHUNK, queries, width), bf16),
             pltpu.VMEM((rows, docs), f32),

time: 41.9 us -> 38 us (0.907)
  Pallas kernels: 39.2 us -> 35.4 us
    pallas_call x1, Pallas kernels: 39.2 us -> 35.4 us  [in_one_kernel(): pl.pallas_call(functools.partial(kernel, nz), out_shape=jax.ShapeDtypeStr...]
where the time goes in v4:
time: 38 us; the launch traced here: 37.8 us
  Pallas kernels  35.4 us (93%)
  other arithmetic  1.68 us (4%)
  between operations  0.67 us (2%)
    pallas_call x1, Pallas kernels, in_one_kernel(): pl.pallas_call(functools.partial(kernel, nz), out_shape=jax.ShapeDtypeStr...  35.4 us
    select_n x1, other arithmetic, in_one_kernel(): return jnp.where(live_slots[None, :], summed, jnp.zeros_like(summed))  1.67 us

profile of v4, /device:TPU:24, one launch (start us, length us, event | category | flops | bytes accessed | tf_op | source)
XLA Modules:
  0.0 37.8 jit_solution(17213837632441213488)
XLA Ops:
  0.7 35.4 %shard_map.73 = f32[64,1024]{1,0:T(8,128)} custom-call(bf16[1,32,4096]{2,1,0:T(8,128)(2,1)} %q_ref.1, bf16[1,1024,4096]{2,1,0:T(8,128)(2,1)} %stored_ref.1, f32[1,64,64]{2,1,0:T(8,128)} %bi_ref.1, f32[1,64,64]{2,1,0:T(8,128)} %bo_ref.1, f32[1,64,64]{2,1,0:T(8,128)} %ev_ref.1, s32[1,256]{1,0:T(1,128)} %bitcast.3), custom_call_target="tpu_custom_call" | custom-call | flops 2147483648 | bytes 8388608 | tf_op jit(solution)/shard_map/pallas_call | solution.py:413
  36.1 1.7 %broadcast_select_fusion = f32[64,1024]{1,0:T(8,128)} fusion(f32[64,1024]{1,0:T(8,128)} %shard_map.73, pred[1024]{0:T(1024)(128)(4,1)S(1)} %iota_compare_fusion), kind=kLoop, calls=%fused_computation | loop fusion | flops 65536 | bytes 525312 | tf_op jit(solution)/shard_map/jit(_where)/select_n | solution.py:441
  (1 shorter events, 0.0 us)

commit v5 on v4

--- a/solution.py
+++ b/solution.py
@@ -304,13 +304,13 @@
 
         @pl.when(k < N_CHUNK - 1)
         def _():
-            acc[...] += nt(gath[k, rows, :], st[k])
+            acc[...] += nt(st[k], gath[k, rows, :])
 
         @pl.when(k == N_CHUNK - 1)
         def _():
             def column(n, carry):
                 cols = pl.ds(pl.multiple_of(n * 256, 256), 256)
-                total = acc[:, cols] + nt(gath[k, rows, :], st[k, cols, :])
+                total = (acc[cols, :] + nt(st[k, cols, :], gath[k, rows, :])).T
 
                 @pl.when(p == mine)
                 def _():
@@ -419,7 +419,7 @@
             pltpu.VMEM((depth * query_grads.shape[1] // 128, 128), f32),
             pltpu.VMEM((N_CHUNK, docs, width), bf16),
             pltpu.VMEM((N_CHUNK, queries, width), bf16),
-            pltpu.VMEM((rows, docs), f32),
+            pltpu.VMEM((docs, rows), f32),
             pltpu.VMEM((nz, docs // 256, rows, 256), bf16),
             pltpu.VMEM((layers, docs // 256, rows, 256), bf16),
             pltpu.SemaphoreType.DMA((N_CHUNK,)),

time: 38 us -> 37.9 us (level)
  no operation moved by 1% of the time
where the time goes in v5:
time: 37.9 us; the launch traced here: 37.8 us
  Pallas kernels  35.4 us (93%)
  other arithmetic  1.68 us (4%)
  between operations  0.67 us (2%)
    pallas_call x1, Pallas kernels, in_one_kernel(): pl.pallas_call(functools.partial(kernel, nz), out_shape=jax.ShapeDtypeStr...  35.4 us
    select_n x1, other arithmetic, in_one_kernel(): return jnp.where(live_slots[None, :], summed, jnp.zeros_like(summed))  1.67 us

profile of v5, /device:TPU:24, one launch (start us, length us, event | category | flops | bytes accessed | tf_op | source)
XLA Modules:
  0.0 37.8 jit_solution(14103928425769169403)
XLA Ops:
  0.7 35.4 %shard_map.73 = f32[64,1024]{1,0:T(8,128)} custom-call(bf16[1,32,4096]{2,1,0:T(8,128)(2,1)} %q_ref.1, bf16[1,1024,4096]{2,1,0:T(8,128)(2,1)} %stored_ref.1, f32[1,64,64]{2,1,0:T(8,128)} %bi_ref.1, f32[1,64,64]{2,1,0:T(8,128)} %bo_ref.1, f32[1,64,64]{2,1,0:T(8,128)} %ev_ref.1, s32[1,256]{1,0:T(1,128)} %bitcast.3), custom_call_target="tpu_custom_call" | custom-call | flops 2147483648 | bytes 8388608 | tf_op jit(solution)/shard_map/pallas_call | solution.py:413
  36.1 1.7 %broadcast_select_fusion = f32[64,1024]{1,0:T(8,128)} fusion(f32[64,1024]{1,0:T(8,128)} %shard_map.73, pred[1024]{0:T(1024)(128)(4,1)S(1)} %iota_compare_fusion), kind=kLoop, calls=%fused_computation | loop fusion | flops 65536 | bytes 525312 | tf_op jit(solution)/shard_map/jit(_where)/select_n | solution.py:441
  (1 shorter events, 0.0 us)

commit v6 on v4

--- a/solution.py
+++ b/solution.py
@@ -148,8 +148,8 @@
 
 def kernel(
     nz, q_ref, stored_ref, bi_ref, bo_ref, ev_ref, mask_ref, out_ref,
-    xs, st, gath, acc, sbuf, rbuf,
-    st_sem, recv_sem, up_sem, down_sem, y_sem, rs_send, rs_recv,
+    xs, st, gath, acc, own, sbuf, rbuf,
+    st_sem, recv_sem, up_sem, down_sem, y_sem, rs_send, rs_recv, out_sem,
 ):
     layers = sbuf.shape[0]
     width = st.shape[2]
@@ -274,11 +274,46 @@
             landed(p, 1 - y, k).wait_recv()
             pass_on(p, k)
 
-    def hand_over(p, s, n):
+    def hand_over(p, s, n, half=None):
+        take = pl.ds(0, 64) if half is None else pl.ds(pl.multiple_of(half * 32, 32), 32)
         return pltpu.make_async_remote_copy(
-            src_ref=sbuf.at[s, n], dst_ref=rbuf.at[mine, n], send_sem=rs_send.at[s, n],
-            recv_sem=rs_recv.at[mine, n], device_id={"layer": p}, device_id_type=MESH,
+            src_ref=sbuf.at[s, n, take], dst_ref=rbuf.at[mine, n, take],
+            send_sem=rs_send.at[s, n], recv_sem=rs_recv.at[mine, n],
+            device_id={"layer": p}, device_id_type=MESH,
         )
+
+    def multiply(p, s, k, half=None):
+        count = 64 if half is None else 32
+        at = 0 if half is None else pl.multiple_of(half * 32, 32)
+        rows = pl.ds(pl.multiple_of(p * 64 + at, 32), count)
+        local = pl.ds(at, count)
+
+        @pl.when(k == 0)
+        def _():
+            acc[local, :] = jnp.zeros((count, acc.shape[1]), f32)
+
+        @pl.when(k < N_CHUNK - 1)
+        def _():
+            acc[local, :] += nt(gath[k, rows, :], st[k])
+
+        @pl.when(k == N_CHUNK - 1)
+        def _():
+            def column(n, carry):
+                cols = pl.ds(pl.multiple_of(n * 256, 256), 256)
+                total = acc[local, cols] + nt(gath[k, rows, :], st[k, cols, :])
+
+                @pl.when(p == mine)
+                def _():
+                    own[local, cols] = total
+
+                @pl.when(p != mine)
+                def _():
+                    sbuf[s, n, local, :] = total.astype(bf16)
+                    hand_over(p, s, n, half).start()
+
+                return carry
+
+            lax.fori_loop(0, parts, column, 0)
 
     def compute(t):
         s, k = t // N_CHUNK, t % N_CHUNK
@@ -296,34 +331,7 @@
         def _():
             load(k).wait()
 
-        rows = pl.ds(pl.multiple_of(p * 64, 64), 64)
-
-        @pl.when(k == 0)
-        def _():
-            acc[...] = jnp.zeros_like(acc)
-
-        @pl.when(k < N_CHUNK - 1)
-        def _():
-            acc[...] += nt(gath[k, rows, :], st[k])
-
-        @pl.when(k == N_CHUNK - 1)
-        def _():
-            def column(n, carry):
-                cols = pl.ds(pl.multiple_of(n * 256, 256), 256)
-                total = acc[:, cols] + nt(gath[k, rows, :], st[k, cols, :])
-
-                @pl.when(p == mine)
-                def _():
-                    out_ref[:, cols] = total
-
-                @pl.when(p != mine)
-                def _():
-                    sbuf[s, n] = total.astype(bf16)
-                    hand_over(p, s, n).start()
-
-                return carry
-
-            lax.fori_loop(0, parts, column, 0)
+        multiply(p, s, k)
 
     steps = nz * N_CHUNK
 
@@ -346,11 +354,69 @@
     write_own_rows(q_ref, bi_ref, bo_ref, ev_ref, mask_ref, xs, gath, me, ready, send_rows)
     lead = N_CHUNK * jnp.where((z == 0) | (z == nz - 1), 1, 2)
     lax.fori_loop(N_CHUNK, lead, first, 0)
-    lax.fori_loop(0, steps, body, 0)
+    lax.fori_loop(0, steps - N_CHUNK, body, 0)
+    relay(steps - 1)
+
+    def last(t, carry):
+        own_side, k = t // N_CHUNK == 0, t % N_CHUNK
+        p = plane_at(nz - 1)
+        side = jnp.where(own_side, y, 1 - y)
+
+        @pl.when(jnp.logical_not(own_side | relayed(p, k)))
+        def _():
+            landed(p, 1 - y, k).wait_recv()
+
+        multiply(p, nz - 1, k, side)
+        return carry
+
+    lax.fori_loop(0, 2 * N_CHUNK, last, 0)
+
+    def drain(t, carry):
+        p, k = t // N_CHUNK, t % N_CHUNK
+
+        @pl.when(goes_up(p))
+        def _():
+            up(p, y, k).wait_send()
+
+        @pl.when(goes_down(p))
+        def _():
+            down(p, y, k).wait_send()
+
+        @pl.when(both_columns(p, k) & goes_up(p))
+        def _():
+            up(p, 1 - y, k).wait_send()
+
+        @pl.when(both_columns(p, k) & goes_down(p))
+        def _():
+            down(p, 1 - y, k).wait_send()
+
+        @pl.when(goes_across(p, k))
+        def _():
+            across(p, k).wait_send()
+
+        return carry
+
+    lax.fori_loop(0, steps, drain, 0)
+
+    def drain_scores(t, carry):
+        s, n = t // parts, t % parts
+        p = plane_at(s)
+
+        @pl.when(p != mine)
+        def _():
+            hand_over(p, s, n).wait_send()
+
+        return carry
+
+    lax.fori_loop(0, nz * parts, drain_scores, 0)
+
+    def write(n):
+        cols = pl.ds(n * 256 if isinstance(n, int) else pl.multiple_of(n * 256, 256), 256)
+        return pltpu.make_async_copy(own.at[:, cols], out_ref.at[:, cols], out_sem.at[n])
 
     def collect(n, carry):
         cols = pl.ds(pl.multiple_of(n * 256, 256), 256)
-        total = out_ref[:, cols]
+        total = own[:, cols]
         for step in range(1, layers):
             other = lax.rem(mine + step, layers)
             pltpu.make_async_remote_copy(
@@ -358,49 +424,13 @@
                 recv_sem=rs_recv.at[other, n], device_id={"layer": other}, device_id_type=MESH,
             ).wait_recv()
             total = total + rbuf[other, n].astype(f32)
-        out_ref[:, cols] = total
+        own[:, cols] = total
+        write(n).start()
         return carry
 
     lax.fori_loop(0, parts, collect, 0)
-
-    def drain(t, carry):
-        p, k = t // N_CHUNK, t % N_CHUNK
-
-        @pl.when(goes_up(p))
-        def _():
-            up(p, y, k).wait_send()
-
-        @pl.when(goes_down(p))
-        def _():
-            down(p, y, k).wait_send()
-
-        @pl.when(both_columns(p, k) & goes_up(p))
-        def _():
-            up(p, 1 - y, k).wait_send()
-
-        @pl.when(both_columns(p, k) & goes_down(p))
-        def _():
-            down(p, 1 - y, k).wait_send()
-
-        @pl.when(goes_across(p, k))
-        def _():
-            across(p, k).wait_send()
-
-        return carry
-
-    lax.fori_loop(0, steps, drain, 0)
-
-    def drain_scores(t, carry):
-        s, n = t // parts, t % parts
-        p = plane_at(s)
-
-        @pl.when(p != mine)
-        def _():
-            hand_over(p, s, n).wait_send()
-
-        return carry
-
-    lax.fori_loop(0, nz * parts, drain_scores, 0)
+    for n in range(parts):
+        write(n).wait()
 
 
 def in_one_kernel(nz, query_grads, stored_grads, basis_in, basis_out, eigen_values, layer_mask, doc_counts):
@@ -414,11 +444,12 @@
         functools.partial(kernel, nz),
         out_shape=jax.ShapeDtypeStruct((rows, docs), f32),
         in_specs=[vmem, pl.BlockSpec(memory_space=pltpu.HBM), vmem, vmem, vmem, vmem],
-        out_specs=vmem,
+        out_specs=pl.BlockSpec(memory_space=pl.ANY),
         scratch_shapes=[
             pltpu.VMEM((depth * query_grads.shape[1] // 128, 128), f32),
             pltpu.VMEM((N_CHUNK, docs, width), bf16),
             pltpu.VMEM((N_CHUNK, queries, width), bf16),
+            pltpu.VMEM((rows, docs), f32),
             pltpu.VMEM((rows, docs), f32),
             pltpu.VMEM((nz, docs // 256, rows, 256), bf16),
             pltpu.VMEM((layers, docs // 256, rows, 256), bf16),
@@ -429,6 +460,7 @@
             pltpu.SemaphoreType.DMA((2 * nz, N_CHUNK)),
             pltpu.SemaphoreType.DMA((nz, docs // 256)),
             pltpu.SemaphoreType.DMA((layers, docs // 256)),
+            pltpu.SemaphoreType.DMA((docs // 256,)),
         ],
         compiler_params=pltpu.CompilerParams(
             collective_id=0, has_side_effects=True, vmem_limit_bytes=58 * 1024 * 1024

time: 38 us -> 39.6 us (1.042)
  Pallas kernels: 35.4 us -> 37.1 us
    pallas_call x1, Pallas kernels: 35.4 us -> 37.1 us  [in_one_kernel(): pl.pallas_call(functools.partial(kernel, nz), out_shape=jax.ShapeDtypeStr...]
where the time goes in v6:
time: 39.6 us; the launch traced here: 39.4 us
  Pallas kernels  37.1 us (94%)
  other arithmetic  1.68 us (4%)
  between operations  0.67 us (2%)
    pallas_call x1, Pallas kernels, in_one_kernel(): pl.pallas_call(functools.partial(kernel, nz), out_shape=jax.ShapeDtypeStr...  37.1 us
    select_n x1, other arithmetic, in_one_kernel(): return jnp.where(live_slots[None, :], summed, jnp.zeros_like(summed))  1.67 us

profile of v6, /device:TPU:24, one launch (start us, length us, event | category | flops | bytes accessed | tf_op | source)
XLA Modules:
  0.0 39.4 jit_solution(9907558146739854633)
XLA Ops:
  0.7 37.1 %shard_map.73 = f32[64,1024]{1,0:T(8,128)} custom-call(bf16[1,32,4096]{2,1,0:T(8,128)(2,1)} %q_ref.1, bf16[1,1024,4096]{2,1,0:T(8,128)(2,1)} %stored_ref.1, f32[1,64,64]{2,1,0:T(8,128)} %bi_ref.1, f32[1,64,64]{2,1,0:T(8,128)} %bo_ref.1, f32[1,64,64]{2,1,0:T(8,128)} %ev_ref.1, s32[1,256]{1,0:T(1,128)} %bitcast.3), custom_call_target="tpu_custom_call" | custom-call | flops 2147483648 | bytes 8388608 | tf_op jit(solution)/shard_map/pallas_call | solution.py:443
  37.7 1.7 %broadcast_select_fusion = f32[64,1024]{1,0:T(8,128)} fusion(f32[64,1024]{1,0:T(8,128)} %shard_map.73, pred[1024]{0:T(1024)(128)(4,1)S(1)} %iota_compare_fusion), kind=kLoop, calls=%fused_computation | loop fusion | flops 65536 | bytes 525312 | tf_op jit(solution)/shard_map/jit(_where)/select_n | solution.py:473
  (1 shorter events, 0.0 us)

commit v7 on v4

--- a/solution.py
+++ b/solution.py
@@ -148,8 +148,8 @@
 
 def kernel(
     nz, q_ref, stored_ref, bi_ref, bo_ref, ev_ref, mask_ref, out_ref,
-    xs, st, gath, acc, sbuf, rbuf,
-    st_sem, recv_sem, up_sem, down_sem, y_sem, rs_send, rs_recv,
+    xs, st, gath, acc, own, sbuf, rbuf, hbuf,
+    st_sem, recv_sem, up_sem, down_sem, y_sem, rs_send, rs_recv, h_recv, out_sem,
 ):
     layers = sbuf.shape[0]
     width = st.shape[2]
@@ -274,10 +274,26 @@
             landed(p, 1 - y, k).wait_recv()
             pass_on(p, k)
 
+    chip, core = mine // 2, mine % 2
+    sibling = 2 * chip + 1 - core
+    opposite = 2 * (1 - chip) + core
+
+    def sums_for(p):
+        return p == opposite
+
+    def helps(p):
+        return p == 2 * (1 - chip) + 1 - core
+
     def hand_over(p, s, n):
         return pltpu.make_async_remote_copy(
-            src_ref=sbuf.at[s, n], dst_ref=rbuf.at[mine, n], send_sem=rs_send.at[s, n],
-            recv_sem=rs_recv.at[mine, n], device_id={"layer": p}, device_id_type=MESH,
+            src_ref=sbuf.at[s, n], dst_ref=rbuf.at[chip, n], send_sem=rs_send.at[s, n],
+            recv_sem=rs_recv.at[chip, n], device_id={"layer": p}, device_id_type=MESH,
+        )
+
+    def help_out(s, n):
+        return pltpu.make_async_remote_copy(
+            src_ref=sbuf.at[s, n], dst_ref=hbuf.at[n], send_sem=rs_send.at[s, n],
+            recv_sem=h_recv.at[n], device_id={"layer": sibling}, device_id_type=MESH,
         )
 
     def compute(t):
@@ -314,16 +330,36 @@
 
                 @pl.when(p == mine)
                 def _():
-                    out_ref[:, cols] = total
-
-                @pl.when(p != mine)
+                    own[:, cols] = total
+
+                @pl.when(sums_for(p))
+                def _():
+                    acc[:, cols] = total
+
+                @pl.when(p == sibling)
                 def _():
                     sbuf[s, n] = total.astype(bf16)
                     hand_over(p, s, n).start()
 
+                @pl.when(helps(p))
+                def _():
+                    sbuf[s, n] = total.astype(bf16)
+                    help_out(s, n).start()
+
                 return carry
 
             lax.fori_loop(0, parts, column, 0)
+
+        @pl.when((k == N_CHUNK - 1) & sums_for(p))
+        def _():
+            def add(n, carry):
+                cols = pl.ds(pl.multiple_of(n * 256, 256), 256)
+                help_out(s, n).wait_recv()
+                sbuf[s, n] = (acc[:, cols] + hbuf[n].astype(f32)).astype(bf16)
+                hand_over(p, s, n).start()
+                return carry
+
+            lax.fori_loop(0, parts, add, 0)
 
     steps = nz * N_CHUNK
 
@@ -348,21 +384,6 @@
     lax.fori_loop(N_CHUNK, lead, first, 0)
     lax.fori_loop(0, steps, body, 0)
 
-    def collect(n, carry):
-        cols = pl.ds(pl.multiple_of(n * 256, 256), 256)
-        total = out_ref[:, cols]
-        for step in range(1, layers):
-            other = lax.rem(mine + step, layers)
-            pltpu.make_async_remote_copy(
-                src_ref=sbuf.at[0, n], dst_ref=rbuf.at[other, n], send_sem=rs_send.at[0, n],
-                recv_sem=rs_recv.at[other, n], device_id={"layer": other}, device_id_type=MESH,
-            ).wait_recv()
-            total = total + rbuf[other, n].astype(f32)
-        out_ref[:, cols] = total
-        return carry
-
-    lax.fori_loop(0, parts, collect, 0)
-
     def drain(t, carry):
         p, k = t // N_CHUNK, t % N_CHUNK
 
@@ -401,6 +422,27 @@
         return carry
 
     lax.fori_loop(0, nz * parts, drain_scores, 0)
+
+    def write(n):
+        cols = pl.ds(n * 256 if isinstance(n, int) else pl.multiple_of(n * 256, 256), 256)
+        return pltpu.make_async_copy(own.at[:, cols], out_ref.at[:, cols], out_sem.at[n])
+
+    def collect(n, carry):
+        cols = pl.ds(pl.multiple_of(n * 256, 256), 256)
+        total = own[:, cols]
+        for slot in range(2):
+            pltpu.make_async_remote_copy(
+                src_ref=sbuf.at[0, n], dst_ref=rbuf.at[slot, n], send_sem=rs_send.at[0, n],
+                recv_sem=rs_recv.at[slot, n], device_id={"layer": sibling}, device_id_type=MESH,
+            ).wait_recv()
+            total = total + rbuf[slot, n].astype(f32)
+        own[:, cols] = total
+        write(n).start()
+        return carry
+
+    lax.fori_loop(0, parts, collect, 0)
+    for n in range(parts):
+        write(n).wait()
 
 
 def in_one_kernel(nz, query_grads, stored_grads, basis_in, basis_out, eigen_values, layer_mask, doc_counts):
@@ -414,21 +456,25 @@
         functools.partial(kernel, nz),
         out_shape=jax.ShapeDtypeStruct((rows, docs), f32),
         in_specs=[vmem, pl.BlockSpec(memory_space=pltpu.HBM), vmem, vmem, vmem, vmem],
-        out_specs=vmem,
+        out_specs=pl.BlockSpec(memory_space=pl.ANY),
         scratch_shapes=[
             pltpu.VMEM((depth * query_grads.shape[1] // 128, 128), f32),
             pltpu.VMEM((N_CHUNK, docs, width), bf16),
             pltpu.VMEM((N_CHUNK, queries, width), bf16),
             pltpu.VMEM((rows, docs), f32),
+            pltpu.VMEM((rows, docs), f32),
             pltpu.VMEM((nz, docs // 256, rows, 256), bf16),
-            pltpu.VMEM((layers, docs // 256, rows, 256), bf16),
+            pltpu.VMEM((2, docs // 256, rows, 256), bf16),
+            pltpu.VMEM((docs // 256, rows, 256), bf16),
             pltpu.SemaphoreType.DMA((N_CHUNK,)),
             pltpu.SemaphoreType.DMA((2 * nz, N_CHUNK)),
             pltpu.SemaphoreType.DMA((2 * nz, N_CHUNK)),
             pltpu.SemaphoreType.DMA((2 * nz, N_CHUNK)),
             pltpu.SemaphoreType.DMA((2 * nz, N_CHUNK)),
             pltpu.SemaphoreType.DMA((nz, docs // 256)),
-            pltpu.SemaphoreType.DMA((layers, docs // 256)),
+            pltpu.SemaphoreType.DMA((2, docs // 256)),
+            pltpu.SemaphoreType.DMA((docs // 256,)),
+            pltpu.SemaphoreType.DMA((docs // 256,)),
         ],
         compiler_params=pltpu.CompilerParams(
             collective_id=0, has_side_effects=True, vmem_limit_bytes=58 * 1024 * 1024

time: 38 us -> 39.1 us (1.029)
  Pallas kernels: 35.4 us -> 36.5 us
    pallas_call x1, Pallas kernels: 35.4 us -> 36.5 us  [in_one_kernel(): pl.pallas_call(functools.partial(kernel, nz), out_shape=jax.ShapeDtypeStr...]
where the time goes in v7:
time: 39.1 us; the launch traced here: 38.9 us
  Pallas kernels  36.5 us (93%)
  other arithmetic  1.68 us (4%)
  between operations  0.67 us (2%)
    pallas_call x1, Pallas kernels, in_one_kernel(): pl.pallas_call(functools.partial(kernel, nz), out_shape=jax.ShapeDtypeStr...  36.5 us
    select_n x1, other arithmetic, in_one_kernel(): return jnp.where(live_slots[None, :], summed, jnp.zeros_like(summed))  1.67 us

profile of v7, /device:TPU:24, one launch (start us, length us, event | category | flops | bytes accessed | tf_op | source)
XLA Modules:
  0.0 38.9 jit_solution(15692135020800172968)
XLA Ops:
  0.7 36.5 %shard_map.73 = f32[64,1024]{1,0:T(8,128)} custom-call(bf16[1,32,4096]{2,1,0:T(8,128)(2,1)} %q_ref.1, bf16[1,1024,4096]{2,1,0:T(8,128)(2,1)} %stored_ref.1, f32[1,64,64]{2,1,0:T(8,128)} %bi_ref.1, f32[1,64,64]{2,1,0:T(8,128)} %bo_ref.1, f32[1,64,64]{2,1,0:T(8,128)} %ev_ref.1, s32[1,256]{1,0:T(1,128)} %bitcast.3), custom_call_target="tpu_custom_call" | custom-call | flops 2147483648 | bytes 8388608 | tf_op jit(solution)/shard_map/pallas_call | solution.py:455
  37.2 1.7 %broadcast_select_fusion = f32[64,1024]{1,0:T(8,128)} fusion(f32[64,1024]{1,0:T(8,128)} %shard_map.73, pred[1024]{0:T(1024)(128)(4,1)S(1)} %iota_compare_fusion), kind=kLoop, calls=%fused_computation | loop fusion | flops 65536 | bytes 525312 | tf_op jit(solution)/shard_map/jit(_where)/select_n | solution.py:487
  (1 shorter events, 0.0 us)

commit v8 on v4

--- a/solution.py
+++ b/solution.py
@@ -148,8 +148,8 @@
 
 def kernel(
     nz, q_ref, stored_ref, bi_ref, bo_ref, ev_ref, mask_ref, out_ref,
-    xs, st, gath, acc, sbuf, rbuf,
-    st_sem, recv_sem, up_sem, down_sem, y_sem, rs_send, rs_recv,
+    xs, st, gath, acc, own, sbuf, rbuf,
+    st_sem, recv_sem, up_sem, down_sem, y_sem, rs_send, rs_recv, out_sem,
 ):
     layers = sbuf.shape[0]
     width = st.shape[2]
@@ -314,7 +314,7 @@
 
                 @pl.when(p == mine)
                 def _():
-                    out_ref[:, cols] = total
+                    own[:, cols] = total
 
                 @pl.when(p != mine)
                 def _():
@@ -348,9 +348,52 @@
     lax.fori_loop(N_CHUNK, lead, first, 0)
     lax.fori_loop(0, steps, body, 0)
 
+    def drain(t, carry):
+        p, k = t // N_CHUNK, t % N_CHUNK
+
+        @pl.when(goes_up(p))
+        def _():
+            up(p, y, k).wait_send()
+
+        @pl.when(goes_down(p))
+        def _():
+            down(p, y, k).wait_send()
+
+        @pl.when(both_columns(p, k) & goes_up(p))
+        def _():
+            up(p, 1 - y, k).wait_send()
+
+        @pl.when(both_columns(p, k) & goes_down(p))
+        def _():
+            down(p, 1 - y, k).wait_send()
+
+        @pl.when(goes_across(p, k))
+        def _():
+            across(p, k).wait_send()
+
+        return carry
+
+    lax.fori_loop(0, steps, drain, 0)
+
+    def drain_scores(t, carry):
+        s, n = t // parts, t % parts
+        p = plane_at(s)
+
+        @pl.when(p != mine)
+        def _():
+            hand_over(p, s, n).wait_send()
+
+        return carry
+
+    lax.fori_loop(0, nz * parts, drain_scores, 0)
+
+    def write(n):
+        cols = pl.ds(n * 256 if isinstance(n, int) else pl.multiple_of(n * 256, 256), 256)
+        return pltpu.make_async_copy(own.at[:, cols], out_ref.at[:, cols], out_sem.at[n])
+
     def collect(n, carry):
         cols = pl.ds(pl.multiple_of(n * 256, 256), 256)
-        total = out_ref[:, cols]
+        total = own[:, cols]
         for step in range(1, layers):
             other = lax.rem(mine + step, layers)
             pltpu.make_async_remote_copy(
@@ -358,49 +401,13 @@
                 recv_sem=rs_recv.at[other, n], device_id={"layer": other}, device_id_type=MESH,
             ).wait_recv()
             total = total + rbuf[other, n].astype(f32)
-        out_ref[:, cols] = total
+        own[:, cols] = total
+        write(n).start()
         return carry
 
     lax.fori_loop(0, parts, collect, 0)
-
-    def drain(t, carry):
-        p, k = t // N_CHUNK, t % N_CHUNK
-
-        @pl.when(goes_up(p))
-        def _():
-            up(p, y, k).wait_send()
-
-        @pl.when(goes_down(p))
-        def _():
-            down(p, y, k).wait_send()
-
-        @pl.when(both_columns(p, k) & goes_up(p))
-        def _():
-            up(p, 1 - y, k).wait_send()
-
-        @pl.when(both_columns(p, k) & goes_down(p))
-        def _():
-            down(p, 1 - y, k).wait_send()
-
-        @pl.when(goes_across(p, k))
-        def _():
-            across(p, k).wait_send()
-
-        return carry
-
-    lax.fori_loop(0, steps, drain, 0)
-
-    def drain_scores(t, carry):
-        s, n = t // parts, t % parts
-        p = plane_at(s)
-
-        @pl.when(p != mine)
-        def _():
-            hand_over(p, s, n).wait_send()
-
-        return carry
-
-    lax.fori_loop(0, nz * parts, drain_scores, 0)
+    for n in range(parts):
+        write(n).wait()
 
 
 def in_one_kernel(nz, query_grads, stored_grads, basis_in, basis_out, eigen_values, layer_mask, doc_counts):
@@ -414,11 +421,12 @@
         functools.partial(kernel, nz),
         out_shape=jax.ShapeDtypeStruct((rows, docs), f32),
         in_specs=[vmem, pl.BlockSpec(memory_space=pltpu.HBM), vmem, vmem, vmem, vmem],
-        out_specs=vmem,
+        out_specs=pl.BlockSpec(memory_space=pl.ANY),
         scratch_shapes=[
             pltpu.VMEM((depth * query_grads.shape[1] // 128, 128), f32),
             pltpu.VMEM((N_CHUNK, docs, width), bf16),
             pltpu.VMEM((N_CHUNK, queries, width), bf16),
+            pltpu.VMEM((rows, docs), f32),
             pltpu.VMEM((rows, docs), f32),
             pltpu.VMEM((nz, docs // 256, rows, 256), bf16),
             pltpu.VMEM((layers, docs // 256, rows, 256), bf16),
@@ -429,6 +437,7 @@
             pltpu.SemaphoreType.DMA((2 * nz, N_CHUNK)),
             pltpu.SemaphoreType.DMA((nz, docs // 256)),
             pltpu.SemaphoreType.DMA((layers, docs // 256)),
+            pltpu.SemaphoreType.DMA((docs // 256,)),
         ],
         compiler_params=pltpu.CompilerParams(
             collective_id=0, has_side_effects=True, vmem_limit_bytes=58 * 1024 * 1024

time: 38 us -> 37.2 us (0.979)
  Pallas kernels: 35.4 us -> 34.7 us
    pallas_call x1, Pallas kernels: 35.4 us -> 34.7 us  [in_one_kernel(): pl.pallas_call(functools.partial(kernel, nz), out_shape=jax.ShapeDtypeStr...]
where the time goes in v8:
time: 37.2 us; the launch traced here: 37 us
  Pallas kernels  34.7 us (93%)
  other arithmetic  1.68 us (5%)
  between operations  0.67 us (2%)
    pallas_call x1, Pallas kernels, in_one_kernel(): pl.pallas_call(functools.partial(kernel, nz), out_shape=jax.ShapeDtypeStr...  34.7 us
    select_n x1, other arithmetic, in_one_kernel(): return jnp.where(live_slots[None, :], summed, jnp.zeros_like(summed))  1.67 us

profile of v8, /device:TPU:24, one launch (start us, length us, event | category | flops | bytes accessed | tf_op | source)
XLA Modules:
  0.0 37.0 jit_solution(8906033383986808381)
XLA Ops:
  0.7 34.7 %shard_map.73 = f32[64,1024]{1,0:T(8,128)} custom-call(bf16[1,32,4096]{2,1,0:T(8,128)(2,1)} %q_ref.1, bf16[1,1024,4096]{2,1,0:T(8,128)(2,1)} %stored_ref.1, f32[1,64,64]{2,1,0:T(8,128)} %bi_ref.1, f32[1,64,64]{2,1,0:T(8,128)} %bo_ref.1, f32[1,64,64]{2,1,0:T(8,128)} %ev_ref.1, s32[1,256]{1,0:T(1,128)} %bitcast.3), custom_call_target="tpu_custom_call" | custom-call | flops 2147483648 | bytes 8388608 | tf_op jit(solution)/shard_map/pallas_call | solution.py:420
  35.3 1.7 %broadcast_select_fusion = f32[64,1024]{1,0:T(8,128)} fusion(f32[64,1024]{1,0:T(8,128)} %shard_map.73, pred[1024]{0:T(1024)(128)(4,1)S(1)} %iota_compare_fusion), kind=kLoop, calls=%fused_computation | loop fusion | flops 65536 | bytes 525312 | tf_op jit(solution)/shard_map/jit(_where)/select_n | solution.py:450
  (1 shorter events, 0.0 us)

commit v9 on v8

--- a/solution.py
+++ b/solution.py
@@ -7,7 +7,7 @@
 from jax.sharding import PartitionSpec as P
 
 damping = 0.1
-N_CHUNK = 4
+N_CHUNK = 8
 MESH = pl.DeviceIdType.MESH
 f32 = jnp.float32
 bf16 = jnp.bfloat16
@@ -137,8 +137,8 @@
     ready()
 
     def chunk(k, carry):
-        for j in range(8):
-            tile = xs[pl.ds(pl.multiple_of(256 * k + 32 * j, 32), 32), :]
+        for j in range(32 // N_CHUNK):
+            tile = xs[pl.ds(pl.multiple_of((1024 // N_CHUNK) * k + 32 * j, 32), 32), :]
             gath[k, rows, 128 * j : 128 * j + 128] = (tile * weights).astype(bf16)
         send_rows(k)
         return carry
@@ -336,9 +336,9 @@
         def _():
             forward(t + lead)
 
-        @pl.when(t + 2 < steps)
-        def _():
-            relay(t + 2)
+        @pl.when(t + N_CHUNK // 2 < steps)
+        def _():
+            relay(t + N_CHUNK // 2)
 
         compute(t)
         return carry

time: 37.2 us -> 41.2 us (1.11)
  Pallas kernels: 34.7 us -> 38.7 us
    pallas_call x1, Pallas kernels: 34.7 us -> 38.7 us  [in_one_kernel(): pl.pallas_call(functools.partial(kernel, nz), out_shape=jax.ShapeDtypeStr...]
where the time goes in v9:
time: 41.2 us; the launch traced here: 41.1 us
  Pallas kernels  38.7 us (94%)
  other arithmetic  1.68 us (4%)
  between operations  0.67 us (2%)
    pallas_call x1, Pallas kernels, in_one_kernel(): pl.pallas_call(functools.partial(kernel, nz), out_shape=jax.ShapeDtypeStr...  38.7 us
    select_n x1, other arithmetic, in_one_kernel(): return jnp.where(live_slots[None, :], summed, jnp.zeros_like(summed))  1.67 us

profile of v9, /device:TPU:24, one launch (start us, length us, event | category | flops | bytes accessed | tf_op | source)
XLA Modules:
  0.0 41.1 jit_solution(11784449671852931826)
XLA Ops:
  0.7 38.7 %shard_map.73 = f32[64,1024]{1,0:T(8,128)} custom-call(bf16[1,32,4096]{2,1,0:T(8,128)(2,1)} %q_ref.1, bf16[1,1024,4096]{2,1,0:T(8,128)(2,1)} %stored_ref.1, f32[1,64,64]{2,1,0:T(8,128)} %bi_ref.1, f32[1,64,64]{2,1,0:T(8,128)} %bo_ref.1, f32[1,64,64]{2,1,0:T(8,128)} %ev_ref.1, s32[1,256]{1,0:T(1,128)} %bitcast.3), custom_call_target="tpu_custom_call" | custom-call | flops 2147483648 | bytes 8388608 | tf_op jit(solution)/shard_map/pallas_call | solution.py:420
  39.4 1.7 %broadcast_select_fusion = f32[64,1024]{1,0:T(8,128)} fusion(f32[64,1024]{1,0:T(8,128)} %shard_map.73, pred[1024]{0:T(1024)(128)(4,1)S(1)} %iota_compare_fusion), kind=kLoop, calls=%fused_computation | loop fusion | flops 65536 | bytes 525312 | tf_op jit(solution)/shard_map/jit(_where)/select_n | solution.py:450
  (1 shorter events, 0.0 us)
